TPU v7x, 32 devices: a whole 2x2x4 slice. The times are simulated.
32 devices in a mesh: pb: 4 (over y, core), ka: 2 (over x), ha: 4 (over z).
Axes of the slice: x: 2, y: 2, z: 4, core: 2. Of those that a mesh axis runs over, the one named last changes fastest.
Arguments:
- queries: bfloat16 [2048, 512], P(('pb', 'ka'), 'ha'), may hold values from -6 to 6
- key_rows: bfloat16 [2048, 512], P(('pb', 'ka'), 'ha'), may hold values from -6 to 6
- value_rows: bfloat16 [2048, 512], P(('pb', 'ka'), 'ha'), may hold values from -6 to 6
- outputs: bfloat16 [2048, 512], P(('pb', 'ka'), 'ha'), may hold values from -6 to 6
- out_grad: bfloat16 [2048, 512], P(('pb', 'ka'), 'ha'), may hold values from -6 to 6
- saved_lse: bfloat16 [2048, 4], P(('pb', 'ka'), 'ha'), may hold values from -1 to 12, as said below
- fold_map: int32 [16], replicated, may hold values from 0 to 15, as said below
Outputs:
- query_grad: bfloat16 [2048, 512], P(('pb', 'ka'), 'ha')
- key_grad: bfloat16 [2048, 512], P(('pb', 'ka'), 'ha')
- value_grad: bfloat16 [2048, 512], P(('pb', 'ka'), 'ha')
Inputs may be any that keep to these rules, and one draw needn't show every extreme that they name: `fold_map`: stored blocks 2 d and 2 d + 1 hold a mirrored pair of blocks, b and 15 - b, in either order; every block is held once. `saved_lse`: close to the log-sum-exp of the row's visible scores.
All inputs are finite; a program needn't handle non-finite values.
Results may differ from a plain program's by a relative error of at most 0.0055.
Values may be sent and summed in bfloat16 or wider, within the bound.
A program may use at most 64 MiB of HBM per device.

v0:
```python
import math

import jax
import jax.numpy as jnp
from jax import lax
from jax.sharding import PartitionSpec as P


def block_length(row_total):
    length = row_total
    while length > 512 and length % 2 == 0:
        length = length // 2
    return length


def tile_grads(
    query_blk, grad_blk, lse_blk, delta_blk, query_pos, key_blk, value_blk, key_pos, factor
):
    scores = (
        jnp.einsum("qhd,khd->hqk", query_blk, key_blk, preferred_element_type=jnp.float32) * factor
    )
    visible = key_pos[None, :] <= query_pos[:, None]
    probs = jnp.where(visible[None], jnp.exp(scores - lse_blk.T[:, :, None]), 0.0)
    probs_low = probs.astype(jnp.bfloat16)
    value_part = jnp.einsum("hqk,qhd->khd", probs_low, grad_blk, preferred_element_type=jnp.float32)
    dprobs = jnp.einsum("qhd,khd->hqk", grad_blk, value_blk, preferred_element_type=jnp.float32)
    dscores = (probs * (dprobs - delta_blk.T[:, :, None])).astype(jnp.bfloat16)
    query_part = jnp.einsum("hqk,khd->qhd", dscores, key_blk, preferred_element_type=jnp.float32)
    key_part = jnp.einsum("hqk,qhd->khd", dscores, query_blk, preferred_element_type=jnp.float32)
    return (query_part, key_part, value_part)


def add_rows(target, update, first_row):
    length = update.shape[0]
    current = lax.dynamic_slice_in_dim(target, first_row, length, 0)
    return lax.dynamic_update_slice_in_dim(target, current + update, first_row, 0)


def body(queries, key_rows, value_rows, outputs, out_grad, saved_lse, fold_map):
    row_count, full_width = queries.shape
    head_count = saved_lse.shape[1]
    head_dim = full_width // head_count
    factor = 1.0 / math.sqrt(head_dim)
    fold_rows = row_count // 2
    size_pb = lax.axis_size("pb")
    size_ka = lax.axis_size("ka")
    index_pb = lax.axis_index("pb")
    index_ka = lax.axis_index("ka")
    key_all, value_all = (
        lax.all_gather(key_rows, "pb", axis=0, tiled=True),
        lax.all_gather(value_rows, "pb", axis=0, tiled=True),
    )
    key_len = size_pb * row_count
    key_all = key_all.reshape(key_len, head_count, head_dim)
    value_all = value_all.reshape(key_len, head_count, head_dim)
    key_iota = jnp.arange(key_len, dtype=jnp.int32)
    key_global = (key_iota // row_count * size_ka + index_ka) * row_count + key_iota % row_count
    key_pos = fold_map[key_global // fold_rows] * fold_rows + key_global % fold_rows
    query_len = size_ka * row_count
    query_first = index_pb * query_len
    query_empty = jnp.zeros((query_len, head_count, head_dim), jnp.float32)
    key_empty = jnp.zeros((key_len, head_count, head_dim), jnp.float32)
    init = (query_empty, key_empty, key_empty)
    query_src = lax.all_gather(queries, "ka", axis=0, tiled=True)
    grad_src = lax.all_gather(out_grad, "ka", axis=0, tiled=True)
    saved_src = lax.all_gather(outputs, "ka", axis=0, tiled=True)
    lse_src = lax.all_gather(saved_lse, "ka", axis=0, tiled=True)
    piece_rows = query_src.shape[0]
    step_rows = block_length(piece_rows)

    def one_block(number, state):
        dq_all, dk_all, dv_all = state
        offset = number * step_rows
        query_blk = lax.dynamic_slice_in_dim(query_src, offset, step_rows, 0).reshape(
            step_rows, head_count, head_dim
        )
        grad_blk = lax.dynamic_slice_in_dim(grad_src, offset, step_rows, 0).reshape(
            step_rows, head_count, head_dim
        )
        lse_blk = lax.dynamic_slice_in_dim(lse_src, offset, step_rows, 0).astype(jnp.float32)
        saved_blk = lax.dynamic_slice_in_dim(saved_src, offset, step_rows, 0).reshape(
            step_rows, head_count, head_dim
        )
        delta_low = jnp.einsum(
            "qhd,qhd->qh", grad_blk, saved_blk, preferred_element_type=jnp.float32
        ).astype(jnp.bfloat16)
        delta_blk = lax.optimization_barrier(delta_low).astype(jnp.float32)
        row_global = query_first + offset + jnp.arange(step_rows, dtype=jnp.int32)
        query_pos = fold_map[row_global // fold_rows] * fold_rows + row_global % fold_rows
        dq_blk, dk_part, dv_part = tile_grads(
            query_blk, grad_blk, lse_blk, delta_blk, query_pos, key_all, value_all, key_pos, factor
        )
        dk_all = dk_all + dk_part
        dv_all = dv_all + dv_part
        dq_all = add_rows(dq_all, dq_blk, offset)
        return (dq_all, dk_all, dv_all)

    dq_all, dk_all, dv_all = lax.fori_loop(0, piece_rows // step_rows, one_block, init)
    query_mine = lax.psum_scatter(
        dq_all.reshape(query_len, full_width), "ka", scatter_dimension=0, tiled=True
    )
    query_grad = (query_mine * factor).astype(jnp.bfloat16)
    key_flat = dk_all.reshape(key_len, full_width)
    value_flat = dv_all.reshape(key_len, full_width)
    key_total, value_total = lax.psum((key_flat, value_flat), "pb")
    key_mine = lax.dynamic_slice_in_dim(key_total, index_pb * row_count, row_count, 0)
    value_mine = lax.dynamic_slice_in_dim(value_total, index_pb * row_count, row_count, 0)
    key_grad = (key_mine * factor).astype(jnp.bfloat16)
    value_grad = value_mine.astype(jnp.bfloat16)
    return (query_grad, key_grad, value_grad)


def solution(mesh):
    return jax.shard_map(
        body,
        mesh=mesh,
        in_specs=(
            P(("pb", "ka"), "ha"),
            P(("pb", "ka"), "ha"),
            P(("pb", "ka"), "ha"),
            P(("pb", "ka"), "ha"),
            P(("pb", "ka"), "ha"),
            P(("pb", "ka"), "ha"),
            P(),
        ),
        out_specs=(P(("pb", "ka"), "ha"), P(("pb", "ka"), "ha"), P(("pb", "ka"), "ha")),
        check_vma=False,
    )
```

profile of v0, /device:TPU:0, one launch (start us, length us, event | category | flops | bytes accessed | tf_op | source)
XLA Modules:
  0.0 113.3 jit_solution(6467487853603763836)
XLA Ops:
  8.0 0.0 all-reduce.3.cloned.1.call-start
  8.0 0.1 compare_reduce_fusion
  8.1 0.1 compare_reduce_fusion.2
  8.2 0.1 compare_reduce_fusion.4
  8.3 0.1 compare_reduce_fusion.6
  8.3 0.1 compare_reduce_fusion.8
  8.6 2.0 %fusion.22 = (s32[1]{0:T(128)}, s32[1]{0:T(128)}, s32[1]{0:T(128)}, s32[1]{0:T(128)}, s32[1]{0:T(128)}, /*index=5*/s32[1]{0:T(128)}, s32[1]{0:T(128)}, s32[1]{0:...) fusion(s32[16]{0:T(128)} %param.13), kind=kLoop, calls=%fused_computation.85 | loop fusion | bytes 128 | tf_op jit(solution)/shard_map/gather | solution.py:58
  10.5 4.4 %compare_select_fusion.1 = s32[1024,1]{0,1:T(1,128)S(1)} fusion(s32[]{:T(128)} %bitcast.9, s32[]{:T(128)} %bitcast.10, s32[]{:T(128)} %bitcast.11, s32[]{:T(128)} %bitcast.12, s32[]{:T(128)} %bitcast.13, s32[]{:T(128)} %bitcast.15, s32[]{:T(128)} %bitcast.14, s32[]{:T(128)S(6)} %axis_index.25), kind=kLoop, calls=%fused_computation.19 | loop fusion | flops 47104 | bytes 4128 | tf_op jit(solution)/shard_map/gather | solution.py:58
  14.9 4.4 %compare_select_fusion.11 = s32[512,1]{0,1:T(1,128)S(1)} fusion(s32[]{:T(128)} %bitcast.9, s32[]{:T(128)} %bitcast.10, s32[]{:T(128)} %bitcast.11, s32[]{:T(128)} %bitcast.12, s32[]{:T(128)} %bitcast.13, s32[]{:T(128)} %bitcast.15, s32[]{:T(128)} %bitcast.14, s32[]{:T(128)S(6)} %mul.86), kind=kLoop, calls=%fused_computation.51 | loop fusion | flops 15872 | bytes 2080 | tf_op jit(solution)/shard_map/while/body/eval_jaxpr/gather | solution.py:89
  19.3 6.1 %all_gather.18 = bf16[512,128]{1,0:T(8,128)(2,1)S(1)} all-gather(bf16[256,128]{1,0:T(8,128)(2,1)} %param.7), channel_id=1, replica_groups=mesh['pb'=4,'ka'=2,'ha'=4] {'ka'}, dimensions={0}, use_global_device_ids=true | all-gather | bytes 196608 | tf_op jit(solution)/shard_map/all_gather | solution.py:64
  25.4 6.5 %all_gather.19 = bf16[1024,128]{1,0:T(8,128)(2,1)S(1)} all-gather(bf16[256,128]{1,0:T(8,128)(2,1)} %param.8), channel_id=1, replica_groups=mesh['pb'=4,'ka'=2,'ha'=4] {'pb'}, dimensions={0}, use_global_device_ids=true | all-gather | bytes 327680 | tf_op jit(solution)/shard_map/all_gather | solution.py:50
  31.9 4.4 %all_gather.20 = bf16[512,1]{0,1:T(2,128)(2,1)S(1)} all-gather(bf16[256,1]{0,1:T(2,128)(2,1)} %param.12), channel_id=1, replica_groups=mesh['pb'=4,'ka'=2,'ha'=4] {'ka'}, dimensions={0}, use_global_device_ids=true | all-gather | bytes 1536 | tf_op jit(solution)/shard_map/all_gather | solution.py:67
  36.3 5.1 %all_gather.21 = bf16[512,128]{1,0:T(8,128)(2,1)S(1)} all-gather(bf16[256,128]{1,0:T(8,128)(2,1)} %param.11), channel_id=1, replica_groups=mesh['pb'=4,'ka'=2,'ha'=4] {'ka'}, dimensions={0}, use_global_device_ids=true | all-gather | bytes 196608 | tf_op jit(solution)/shard_map/all_gather | solution.py:65
  41.5 6.0 %all_gather.22 = bf16[1024,128]{1,0:T(8,128)(2,1)S(1)} all-gather(bf16[256,128]{1,0:T(8,128)(2,1)} %param.9), channel_id=1, replica_groups=mesh['pb'=4,'ka'=2,'ha'=4] {'pb'}, dimensions={0}, use_global_device_ids=true | all-gather | bytes 327680 | tf_op jit(solution)/shard_map/all_gather | solution.py:51
  47.5 5.2 %all_gather.23 = bf16[512,128]{1,0:T(8,128)(2,1)S(1)} all-gather(bf16[256,128]{1,0:T(8,128)(2,1)} %param.10), channel_id=1, replica_groups=mesh['pb'=4,'ka'=2,'ha'=4] {'ka'}, dimensions={0}, use_global_device_ids=true | all-gather | bytes 196608 | tf_op jit(solution)/shard_map/all_gather | solution.py:66
  52.7 0.2 fusion.2
  52.9 5.7 %fusion.15 = s32[1024]{0:T(1024)S(1)} fusion(pred[1024]{0:T(1024)(128)(4,1)S(1)} %get-tuple-element.61, pred[1024]{0:T(1024)(128)(4,1)S(1)} %get-tuple-element.62, pred[1024]{0:T(1024)(128)(4,1)S(1)} %get-tuple-element.63, pred[1024]{0:T(1024)(128)(4,1)S(1)} %get-tuple-element.64, pred[1024]{0:T(1024)(128)(4,1)S(1)} %get-tuple-element.65, ...), kind=kLoop, calls=%fused_computation.73 | loop fusion | flops 38912 | bytes 17448 | tf_op jit(solution)/shard_map/add | solution.py:58
  58.6 5.7 %fusion.21 = s32[512]{0:T(512)S(1)} fusion(pred[512]{0:T(512)(128)(4,1)S(1)} %get-tuple-element.69, pred[512]{0:T(512)(128)(4,1)S(1)} %get-tuple-element.70, pred[512]{0:T(512)(128)(4,1)S(1)} %get-tuple-element.71, pred[512]{0:T(512)(128)(4,1)S(1)} %get-tuple-element.72, pred[512]{0:T(512)(128)(4,1)S(1)} %get-tuple-element.73, ...), kind=kLoop, calls=%fused_computation.83 | loop fusion | flops 11776 | bytes 8744 | tf_op jit(solution)/shard_map/while/body/eval_jaxpr/add | solution.py:89
  64.3 0.6 exponential_select_fusion
  64.9 0.4 multiply_convert_fusion
  65.3 1.3 %fusion.24 = f32[1024,128]{1,0:T(8,128)} fusion(bf16[512,1024]{1,0:T(8,128)(2,1)S(1)} %multiply_convert_fusion, bf16[512,128]{1,0:T(8,128)(2,1)S(1)} %all_gather.18), kind=kOutput, calls=%fused_computation.87 | convolution fusion | flops 134217728 | bytes 1703936 | tf_op jit(solution)/shard_map/while/body/eval_jaxpr/hqk,qhd->khd/dot_general | solution.py:29
  66.6 0.0 all-reduce.3.cloned.1.call-update
  66.7 0.0 reduce-scatter.2.cloned.1.call-start
  66.7 1.2 %fusion.23 = f32[512,128]{1,0:T(8,128)} fusion(bf16[512,1024]{1,0:T(8,128)(2,1)S(1)} %multiply_convert_fusion, bf16[1024,128]{1,0:T(8,128)(2,1)S(1)} %all_gather.19), kind=kOutput, calls=%fused_computation.86 | convolution fusion | flops 134217728 | bytes 1572864 | tf_op jit(solution)/shard_map/while/body/eval_jaxpr/hqk,khd->qhd/dot_general | solution.py:28
  67.9 0.0 reduce-scatter.2.cloned.1.call-update
  67.9 0.5 fusion
  68.4 18.8 %all-reduce.4 = bf16[1024,128]{1,0:T(8,128)(2,1)S(1)} all-reduce(f32[1024,128]{1,0:T(8,128)S(1)} %fusion), channel_id=1, replica_groups=mesh['pb'=4,'ka'=2,'ha'=4] {'pb'}, use_global_device_ids=true, to_apply=%region_2.3 | all-reduce | flops 131072 | bytes 786432 | tf_op jit(solution)/shard_map/psum | solution.py:105
  87.2 0.6 dynamic-slice_convert_fusion
  87.8 15.0 %all-reduce.3.cloned.1.call-done = f32[1024,128]{1,0:T(8,128)} async-done(((f32[1024,128]{1,0:T(8,128)}), f32[1024,128]{1,0:T(8,128)}) %all-reduce.3.cloned.1.call-update) | async-done | bytes 524304 | tf_op jit(solution)/shard_map/psum | solution.py:105
  102.8 1.5 %multiply_convert_fusion.1 = bf16[256,128]{1,0:T(8,128)(2,1)} fusion(f32[1024,128]{1,0:T(8,128)} %all-reduce.3.cloned.1.call-done, s32[]{:T(128)S(6)} %select_n.130), kind=kLoop, calls=%fused_computation.7 | loop fusion | flops 65536 | bytes 196612 | tf_op jit(solution)/shard_map/convert_element_type | solution.py:108
  104.3 0.0 reduce-scatter.2.cloned.1.call-done
  104.3 1.5 %multiply_convert_fusion.2 = bf16[256,128]{1,0:T(8,128)(2,1)} fusion(f32[256,128]{1,0:T(8,128)} %reduce-scatter.2.cloned.1.call-done), kind=kLoop, calls=%fused_computation.8 | loop fusion | flops 65536 | bytes 196608 | tf_op jit(solution)/shard_map/convert_element_type | solution.py:102
  (8 shorter events, 0.2 us)
Async XLA Ops:
  8.0 94.8 %all-reduce.3.cloned.1.call-start = ((), (), s32[]{:S(2)}) async-start(), calls=%async_computation.2 | async-start | bytes 1048576 | tf_op jit(solution)/shard_map/psum | solution.py:105
  66.7 37.7 %reduce-scatter.2.cloned.1.call-start = ((), (), s32[]{:S(2)}) async-start(), calls=%async_computation.1 | async-start | bytes 393216 | tf_op jit(solution)/shard_map/reduce_scatter | solution.py:99
Sparse Core Ops, SparseCore 0:
  66.8 35.9 all-reduce.2
Sparse Core Ops, SparseCore 1:
  69.3 12.8 reduce-scatter.1
where the time goes:
time: 114 us; the launch traced here: 113 us
  blocking collectives  52.2 us (46%)
  other arithmetic  23.9 us (21%)
  between operations  15.6 us (14%)
  waiting for transfers between devices  15 us (13%)
  matrix products  3.95 us (3%)
  local copies, waits for them, and re-layouts  2.61 us (2%)
    psum x1, blocking collectives, body(): key_total, value_total = lax.psum((key_flat, value_flat), 'pb')  18.8 us
    psum x1, waiting for transfers between devices, body(): key_total, value_total = lax.psum((key_flat, value_flat), 'pb')  15 us
    all_gather x1, blocking collectives, body(): lax.all_gather(key_rows, 'pb', axis=0, tiled=True)  6.46 us
    all_gather x1, blocking collectives, body(): query_src = lax.all_gather(queries, 'ka', axis=0, tiled=True)  6.11 us
    all_gather x1, blocking collectives, body(): lax.all_gather(value_rows, 'pb', axis=0, tiled=True)  5.98 us
    add x1, other arithmetic, body(): fold_map[key_global // fold_rows] * fold_rows + key_global % fold_rows  5.71 us
    add x1, other arithmetic, one_block(): fold_map[row_global // fold_rows] * fold_rows + row_global % fold_rows  5.71 us
    all_gather x1, blocking collectives, body(): saved_src = lax.all_gather(outputs, 'ka', axis=0, tiled=True)  5.22 us
  transfers between devices with their start and end apart: 2, of which 1 were waited for; matrix products, arithmetic and copies ran while one was open for 3% of the time, Pallas kernels for 0%

commit v1 on v0

--- a/solution.py
+++ b/solution.py
@@ -1,8 +1,11 @@
+import functools
 import math
 
 import jax
 import jax.numpy as jnp
 from jax import lax
+from jax.experimental import pallas as pl
+from jax.experimental.pallas import tpu as pltpu
 from jax.sharding import PartitionSpec as P
 
 
@@ -110,9 +113,201 @@
     return (query_grad, key_grad, value_grad)
 
 
+MESH = pl.DeviceIdType.MESH
+NT = (((1,), (1,)), ((), ()))
+TN = (((0,), (0,)), ((), ()))
+
+
+def plane_kernel(
+    rows, factor,
+    q_in, k_in, v_in, o_in, g_in, lse_in, map_in,
+    dq_out, dk_out, dv_out,
+    q_buf, g_buf, k_buf, v_buf, o_buf, lse_buf, map_buf, stat,
+    dq_acc, dk_acc, dv_acc,
+    kv_send, kv_recv, qc_send, qc_recv, qx_send, qx_recv,
+    local_sem, send_sem, recv_sem,
+):
+    p = lax.axis_index("pb")
+    x = lax.axis_index("ka")
+    h = lax.axis_index("ha")
+    c = lax.rem(p, 2)
+    y = p // 2
+    p_core = p + 1 - 2 * c
+    p_far = lax.rem(p + 2, 4)
+    to_core = (p_core, x, h)
+    to_x = (p, 1 - x, h)
+    to_y = (p_far, x, h)
+    to_both = (p_core, 1 - x, h)
+    fold_rows = rows // 2
+
+    def part(slot):
+        return pl.ds(slot * rows, rows)
+
+    locals_ = []
+    for n, (src, dst) in enumerate((
+        (g_in, g_buf.at[part(0)]), (o_in, o_buf), (lse_in, lse_buf), (q_in, q_buf.at[part(0)]),
+        (k_in, k_buf.at[part(0)]), (v_in, v_buf.at[part(0)]), (map_in, map_buf),
+    )):
+        copy = pltpu.make_async_copy(src, dst, local_sem.at[n])
+        copy.start()
+        locals_.append(copy)
+
+    barrier = pltpu.get_barrier_semaphore()
+    for peer in (to_core, to_x, to_y, to_both):
+        pl.semaphore_signal(barrier, inc=1, device_id=peer, device_id_type=MESH)
+    pl.semaphore_wait(barrier, 4)
+
+    sends = []
+
+    def send(n, src, dst, peer):
+        copy = pltpu.make_async_remote_copy(
+            src_ref=src, dst_ref=dst, send_sem=send_sem.at[n], recv_sem=recv_sem.at[n],
+            device_id=peer, device_id_type=MESH,
+        )
+        copy.start()
+        sends.append(copy)
+        return copy
+
+    q_x = send(0, q_in, q_buf.at[part(2)], to_x)
+    k_y = send(1, k_in, k_buf.at[part(1)], to_y)
+    q_c = send(2, q_in, q_buf.at[part(1)], to_core)
+    g_c = send(3, g_in, g_buf.at[part(1)], to_core)
+    g_x = send(4, g_in, g_buf.at[part(2)], to_x)
+    v_y = send(5, v_in, v_buf.at[part(1)], to_y)
+
+    for copy in locals_[:3]:
+        copy.wait()
+    gram = lax.dot_general(o_buf[...], g_buf[part(0)], NT, preferred_element_type=jnp.float32)
+    down = lax.broadcasted_iota(jnp.int32, (rows, rows), 0)
+    along = lax.broadcasted_iota(jnp.int32, (rows, rows), 1)
+    delta = jnp.sum(jnp.where(down == along, gram, 0.0), axis=0, keepdims=True)
+    delta = delta.astype(jnp.bfloat16).astype(jnp.float32)
+    log2e = math.log2(math.e)
+    lse = lse_buf[...].astype(jnp.float32) * log2e
+    which = lax.broadcasted_iota(jnp.int32, (8, rows), 0)
+    stat[0] = jnp.where(which == 0, lse, delta)
+    st_c = send(6, stat.at[0], stat.at[1], to_core)
+    st_x = send(7, stat.at[0], stat.at[2], to_x)
+    st_b = send(8, stat.at[0], stat.at[3], to_both)
+    for copy in locals_[3:]:
+        copy.wait()
+
+    lane = lax.broadcasted_iota(jnp.int32, (1, fold_rows), 1)
+    level = lax.broadcasted_iota(jnp.int32, (fold_rows, 1), 0)
+    q_owner = (p * 2 + x, p_core * 2 + x, p * 2 + 1 - x, p_core * 2 + 1 - x)
+    k_owner = (p * 2 + x, p_far * 2 + x)
+
+    def tile(j, s, first_q, first_k):
+        keys, values = k_buf[part(j)], v_buf[part(j)]
+        query, grad = q_buf[part(s)], g_buf[part(s)]
+        k_pos = jnp.concatenate(
+            [map_buf[k_owner[j] * 2 + i] * fold_rows + level for i in range(2)], axis=0)
+        q_pos = jnp.concatenate(
+            [map_buf[q_owner[s] * 2 + i] * fold_rows + lane for i in range(2)], axis=1)
+        scores = lax.dot_general(keys, query, NT, preferred_element_type=jnp.float32)
+        probs = jnp.where(
+            k_pos <= q_pos, jnp.exp2(scores * (factor * log2e) - stat[s, 0:1, :]), 0.0)
+        dv = jnp.dot(probs.astype(jnp.bfloat16), grad, preferred_element_type=jnp.float32)
+        dprobs = lax.dot_general(values, grad, NT, preferred_element_type=jnp.float32)
+        dscores = (probs * (dprobs - stat[s, 1:2, :])).astype(jnp.bfloat16)
+        dk = jnp.dot(dscores, query, preferred_element_type=jnp.float32)
+        dq = lax.dot_general(dscores, keys, TN, preferred_element_type=jnp.float32)
+        dv_acc[part(j)] = dv if first_k else dv_acc[part(j)] + dv
+        dk_acc[part(j)] = dk if first_k else dk_acc[part(j)] + dk
+        dq_acc[part(s)] = dq if first_q else dq_acc[part(s)] + dq
+
+    tile(0, 0, True, True)
+    q_c.wait_recv()
+    g_c.wait_recv()
+    st_c.wait_recv()
+    tile(0, 1, True, False)
+    q_x.wait_recv()
+    q_r = send(9, q_buf.at[part(2)], q_buf.at[part(3)], to_core)
+    k_y.wait_recv()
+    g_x.wait_recv()
+    g_r = send(10, g_buf.at[part(2)], g_buf.at[part(3)], to_core)
+    v_y.wait_recv()
+    tile(1, 0, False, True)
+    tile(1, 1, False, False)
+    qc_send[0] = dq_acc[part(1)].astype(jnp.bfloat16)
+    dq_c0 = send(11, qc_send.at[0], qc_recv.at[0], to_core)
+    st_x.wait_recv()
+    tile(1, 2, True, False)
+    q_r.wait_recv()
+    g_r.wait_recv()
+    st_b.wait_recv()
+    tile(1, 3, True, False)
+    kv_send[0] = dv_acc[part(1)].astype(jnp.bfloat16)
+    dv_y = send(12, kv_send.at[0], kv_recv.at[0], to_y)
+    kv_send[1] = dk_acc[part(1)].astype(jnp.bfloat16)
+    dk_y = send(13, kv_send.at[1], kv_recv.at[1], to_y)
+    tile(0, 3, False, False)
+    qc_send[1] = dq_acc[part(3)].astype(jnp.bfloat16)
+    dq_c1 = send(14, qc_send.at[1], qc_recv.at[1], to_core)
+    tile(0, 2, False, False)
+    dq_c1.wait_recv()
+    qx_send[...] = (dq_acc[part(2)] + qc_recv[1].astype(jnp.float32)).astype(jnp.bfloat16)
+    dq_x = send(15, qx_send, qx_recv, to_x)
+    dq_c0.wait_recv()
+    dq_mine = dq_acc[part(0)] + qc_recv[0].astype(jnp.float32)
+    dv_y.wait_recv()
+    dv_out[...] = (dv_acc[part(0)] + kv_recv[0].astype(jnp.float32)).astype(jnp.bfloat16)
+    dk_y.wait_recv()
+    dk_out[...] = (
+        (dk_acc[part(0)] + kv_recv[1].astype(jnp.float32)) * factor).astype(jnp.bfloat16)
+    dq_x.wait_recv()
+    dq_out[...] = ((dq_mine + qx_recv[...].astype(jnp.float32)) * factor).astype(jnp.bfloat16)
+    for copy in sends:
+        copy.wait_send()
+
+
+def plane_body(queries, key_rows, value_rows, outputs, out_grad, saved_lse, fold_map):
+    rows, width = queries.shape
+    factor = 1.0 / math.sqrt(width)
+    low, full = jnp.bfloat16, jnp.float32
+    grad = jax.ShapeDtypeStruct((rows, width), low)
+    return pl.pallas_call(
+        functools.partial(plane_kernel, rows, factor),
+        out_shape=(grad, grad, grad),
+        in_specs=[pl.BlockSpec(memory_space=pl.ANY)] * 7,
+        out_specs=[pl.BlockSpec(memory_space=pltpu.VMEM)] * 3,
+        scratch_shapes=[
+            pltpu.VMEM((4 * rows, width), low),
+            pltpu.VMEM((4 * rows, width), low),
+            pltpu.VMEM((2 * rows, width), low),
+            pltpu.VMEM((2 * rows, width), low),
+            pltpu.VMEM((rows, width), low),
+            pltpu.VMEM((1, rows), low),
+            pltpu.SMEM(fold_map.shape, jnp.int32),
+            pltpu.VMEM((4, 8, rows), full),
+            pltpu.VMEM((4 * rows, width), full),
+            pltpu.VMEM((2 * rows, width), full),
+            pltpu.VMEM((2 * rows, width), full),
+            pltpu.VMEM((2, rows, width), low),
+            pltpu.VMEM((2, rows, width), low),
+            pltpu.VMEM((2, rows, width), low),
+            pltpu.VMEM((2, rows, width), low),
+            pltpu.VMEM((rows, width), low),
+            pltpu.VMEM((rows, width), low),
+            pltpu.SemaphoreType.DMA((7,)),
+            pltpu.SemaphoreType.DMA((16,)),
+            pltpu.SemaphoreType.DMA((16,)),
+        ],
+        compiler_params=pltpu.CompilerParams(
+            collective_id=0, has_side_effects=True, vmem_limit_bytes=32 * 2**20
+        ),
+        cost_estimate=pl.CostEstimate(
+            flops=80 * rows * rows * width,
+            bytes_accessed=16 * rows * width,
+            transcendentals=8 * rows * rows,
+        ),
+    )(queries, key_rows, value_rows, outputs, out_grad, saved_lse.reshape(1, rows), fold_map)
+
+
 def solution(mesh):
+    plane = mesh.shape["pb"] == 4 and mesh.shape["ka"] == 2
     return jax.shard_map(
-        body,
+        plane_body if plane else body,
         mesh=mesh,
         in_specs=(
             P(("pb", "ka"), "ha"),

time: 114 us -> 23.3 us (0.20)
  blocking collectives: 52.2 us -> 0 us
  other arithmetic: 23.9 us -> 0 us
  Pallas kernels: 0 us -> 15.5 us
  waiting for transfers between devices: 15 us -> 0 us
  between operations: 15.6 us -> 0.66 us
  local copies, waits for them, and re-layouts: 2.61 us -> 6.76 us
  matrix products: 3.95 us -> 0 us
    all_gather x6 -> x0, blocking collectives: 33.4 us -> none  [the longest x1 6.46 us: body(): lax.all_gather(key_rows, 'pb', axis=0, tiled=True)]
    psum x1 -> x0, blocking collectives: 18.8 us -> none  [body(): key_total, value_total = lax.psum((key_flat, value_flat), 'pb')]
    pallas_call x0 -> x1, Pallas kernels: none -> 15.5 us  [plane_body(): pl.pallas_call(functools.partial(plane_kernel, rows, factor), out_shape=(...]
    psum x1 -> x0, waiting for transfers between devices: 15 us -> none  [body(): key_total, value_total = lax.psum((key_flat, value_flat), 'pb')]
    add x2 -> x0, other arithmetic: 11.4 us -> none  [the longest x1 5.71 us: body(): fold_map[key_global // fold_rows] * fold_rows + key_global % fold_rows]
    gather x12 -> x0, other arithmetic: 9.27 us -> none  [the longest x6 4.72 us: body(): fold_map[key_global // fold_rows] * fold_rows + key_global % fold_rows]
    unnamed x0 -> x17, local copies, waits for them, and re-layouts: none -> 6.76 us
    dot_general x5 -> x0, matrix products: 3.95 us -> none  [the longest x1 1.29 us: tile_grads(): jnp.einsum('hqk,qhd->khd', dscores, query_blk, preferred_element_type=jnp...]
  transfers between devices with their start and end apart: 2 -> 0, of which waited for: 1 -> 0; matrix products, arithmetic and copies ran while one was open for 3% -> 0% of each run, Pallas kernels for 0% -> 0%
where the time goes in v1:
time: 23.3 us; the launch traced here: 22.9 us
  Pallas kernels  15.5 us (67%)
  local copies, waits for them, and re-layouts  6.76 us (29%)
  between operations  0.66 us (3%)
    pallas_call x1, Pallas kernels, plane_body(): pl.pallas_call(functools.partial(plane_kernel, rows, factor), out_shape=(...  15.5 us
    unnamed x17, local copies, waits for them, and re-layouts  6.76 us

profile of v1, /device:TPU:0, one launch (start us, length us, event | category | flops | bytes accessed | tf_op | source)
XLA Modules:
  0.0 22.9 jit_solution(2659526238597067403)
XLA Ops:
  0.6 0.0 copy-start.6
  0.6 0.0 copy-start.5
  0.7 0.6 %copy-done.6 = s32[16]{0:T(128)S(1)} copy-done((s32[16]{0:T(128)S(1)}, s32[16]{0:T(128)}, u32[]{:S(2)}) %copy-start.6) | copy-done | bytes 88
  1.3 0.0 copy-done.5
  1.3 0.0 copy-start
  1.3 0.8 %copy-done = bf16[256,128]{1,0:T(8,128)(2,1)S(1)} copy-done((bf16[256,128]{1,0:T(8,128)(2,1)S(1)}, bf16[256,128]{1,0:T(8,128)(2,1)}, u32[]{:S(2)}) %copy-start) | copy-done | bytes 65560
  2.2 0.0 copy-start.1
  2.2 0.8 %copy-done.1 = bf16[256,128]{1,0:T(8,128)(2,1)S(1)} copy-done((bf16[256,128]{1,0:T(8,128)(2,1)S(1)}, bf16[256,128]{1,0:T(8,128)(2,1)}, u32[]{:S(2)}) %copy-start.1) | copy-done | bytes 65560
  3.0 0.0 copy-start.2
  3.0 0.8 %copy-done.2 = bf16[256,128]{1,0:T(8,128)(2,1)S(1)} copy-done((bf16[256,128]{1,0:T(8,128)(2,1)S(1)}, bf16[256,128]{1,0:T(8,128)(2,1)}, u32[]{:S(2)}) %copy-start.2) | copy-done | bytes 65560
  3.8 0.0 copy-start.3
  3.9 0.8 %copy-done.3 = bf16[256,128]{1,0:T(8,128)(2,1)S(1)} copy-done((bf16[256,128]{1,0:T(8,128)(2,1)S(1)}, bf16[256,128]{1,0:T(8,128)(2,1)}, u32[]{:S(2)}) %copy-start.3) | copy-done | bytes 65560
  4.7 0.0 copy-start.4
  4.7 0.8 %copy-done.4 = bf16[256,128]{1,0:T(8,128)(2,1)S(1)} copy-done((bf16[256,128]{1,0:T(8,128)(2,1)S(1)}, bf16[256,128]{1,0:T(8,128)(2,1)}, u32[]{:S(2)}) %copy-start.4) | copy-done | bytes 65560
  5.5 15.5 %shard_map.94 = (bf16[256,128]{1,0:T(8,128)(2,1)S(1)}, bf16[256,128]{1,0:T(8,128)(2,1)S(1)}, bf16[256,128]{1,0:T(8,128)(2,1)S(1)}) custom-call(bf16[256,128]{1,0:T(8,128)(2,1)S(1)} %copy-done, bf16[256,128]{1,0:T(8,128)(2,1)S(1)} %copy-done.1, bf16[256,128]{1,0:T(8,128)(2,1)S(1)} %copy-done.2, bf16[256,128]{1,0:T(8,128)(2,1)S(1)} %copy-done.3, ...), custom_call_target="tpu_custom_call" | custom-call | flops 671088640 | bytes 524288 | tf_op jit(solution)/shard_map/pallas_call | solution.py:269
  21.0 0.6 %copy.13 = bf16[256,128]{1,0:T(8,128)(2,1)} copy(bf16[256,128]{1,0:T(8,128)(2,1)S(1)} %get-tuple-element.6) | data formatting | bytes 131072
  21.7 0.6 %copy.14 = bf16[256,128]{1,0:T(8,128)(2,1)} copy(bf16[256,128]{1,0:T(8,128)(2,1)S(1)} %get-tuple-element.7) | data formatting | bytes 131072
  22.3 0.6 %copy.15 = bf16[256,128]{1,0:T(8,128)(2,1)} copy(bf16[256,128]{1,0:T(8,128)(2,1)S(1)} %get-tuple-element.8) | data formatting | bytes 131072
Async XLA Ops:
  0.6 0.7 %copy-start.6 = (s32[16]{0:T(128)S(1)}, s32[16]{0:T(128)}, u32[]{:S(2)}) copy-start(s32[16]{0:T(128)} %map_in.1) | copy-start | bytes 196
  0.6 0.7 %copy-start.5 = (bf16[256,1]{0,1:T(2,128)(2,1)S(1)}, bf16[256,1]{0,1:T(2,128)(2,1)}, u32[]{:S(2)}) copy-start(bf16[256,1]{0,1:T(2,128)(2,1)} %param.12) | copy-start | bytes 1540
  1.3 0.8 %copy-start = (bf16[256,128]{1,0:T(8,128)(2,1)S(1)}, bf16[256,128]{1,0:T(8,128)(2,1)}, u32[]{:S(2)}) copy-start(bf16[256,128]{1,0:T(8,128)(2,1)} %q_in.1) | copy-start | bytes 196612
  2.2 0.8 %copy-start.1 = (bf16[256,128]{1,0:T(8,128)(2,1)S(1)}, bf16[256,128]{1,0:T(8,128)(2,1)}, u32[]{:S(2)}) copy-start(bf16[256,128]{1,0:T(8,128)(2,1)} %k_in.1) | copy-start | bytes 196612
  3.0 0.8 %copy-start.2 = (bf16[256,128]{1,0:T(8,128)(2,1)S(1)}, bf16[256,128]{1,0:T(8,128)(2,1)}, u32[]{:S(2)}) copy-start(bf16[256,128]{1,0:T(8,128)(2,1)} %v_in.1) | copy-start | bytes 196612
  3.8 0.8 %copy-start.3 = (bf16[256,128]{1,0:T(8,128)(2,1)S(1)}, bf16[256,128]{1,0:T(8,128)(2,1)}, u32[]{:S(2)}) copy-start(bf16[256,128]{1,0:T(8,128)(2,1)} %o_in.1) | copy-start | bytes 196612
  4.7 0.8 %copy-start.4 = (bf16[256,128]{1,0:T(8,128)(2,1)S(1)}, bf16[256,128]{1,0:T(8,128)(2,1)}, u32[]{:S(2)}) copy-start(bf16[256,128]{1,0:T(8,128)(2,1)} %g_in.1) | copy-start | bytes 196612

commit v2 on v1

--- a/solution.py
+++ b/solution.py
@@ -124,8 +124,8 @@
     dq_out, dk_out, dv_out,
     q_buf, g_buf, k_buf, v_buf, o_buf, lse_buf, map_buf, stat,
     dq_acc, dk_acc, dv_acc,
-    kv_send, kv_recv, qc_send, qc_recv, qx_send, qx_recv,
-    local_sem, send_sem, recv_sem,
+    kv_send, kv_recv, dq_send, dq_recv,
+    stage, store_sem, local_sem, send_sem, recv_sem,
 ):
     p = lax.axis_index("pb")
     x = lax.axis_index("ka")
@@ -192,29 +192,56 @@
     for copy in locals_[3:]:
         copy.wait()
 
-    lane = lax.broadcasted_iota(jnp.int32, (1, fold_rows), 1)
-    level = lax.broadcasted_iota(jnp.int32, (fold_rows, 1), 0)
     q_owner = (p * 2 + x, p_core * 2 + x, p * 2 + 1 - x, p_core * 2 + 1 - x)
     k_owner = (p * 2 + x, p_far * 2 + x)
-
-    def tile(j, s, first_q, first_k):
+    half = lax.broadcasted_iota(jnp.int32, (1, rows), 1) // fold_rows
+    lane = lax.broadcasted_iota(jnp.int32, (fold_rows, rows), 1) % fold_rows
+    level = lax.broadcasted_iota(jnp.int32, (fold_rows, rows), 0)
+
+    def probabilities(j, s, scores):
+        q_fold = jnp.where(half == 0, map_buf[q_owner[s] * 2], map_buf[q_owner[s] * 2 + 1])
+        lse_row = stat[s, 0:1, :]
+        parts = []
+        for i in range(2):
+            k_fold = map_buf[k_owner[j] * 2 + i]
+            scaled = scores[i * fold_rows:(i + 1) * fold_rows] * (factor * log2e)
+            if j == 0 and s == 0:
+                seen = k_fold * fold_rows + level <= q_fold * fold_rows + lane
+                parts.append(jnp.where(seen, jnp.exp2(scaled - lse_row), 0.0))
+            else:
+                parts.append(jnp.exp2(scaled - jnp.where(q_fold > k_fold, lse_row, 1e30)))
+        return jnp.concatenate(parts, axis=0)
+
+    def tile(j, s, first_q, first_k, after_dv=None):
         keys, values = k_buf[part(j)], v_buf[part(j)]
         query, grad = q_buf[part(s)], g_buf[part(s)]
-        k_pos = jnp.concatenate(
-            [map_buf[k_owner[j] * 2 + i] * fold_rows + level for i in range(2)], axis=0)
-        q_pos = jnp.concatenate(
-            [map_buf[q_owner[s] * 2 + i] * fold_rows + lane for i in range(2)], axis=1)
         scores = lax.dot_general(keys, query, NT, preferred_element_type=jnp.float32)
-        probs = jnp.where(
-            k_pos <= q_pos, jnp.exp2(scores * (factor * log2e) - stat[s, 0:1, :]), 0.0)
+        dprobs = lax.dot_general(values, grad, NT, preferred_element_type=jnp.float32)
+        probs = probabilities(j, s, scores)
         dv = jnp.dot(probs.astype(jnp.bfloat16), grad, preferred_element_type=jnp.float32)
-        dprobs = lax.dot_general(values, grad, NT, preferred_element_type=jnp.float32)
+        dv_acc[part(j)] = dv if first_k else dv_acc[part(j)] + dv
+        if after_dv is not None:
+            after_dv()
         dscores = (probs * (dprobs - stat[s, 1:2, :])).astype(jnp.bfloat16)
         dk = jnp.dot(dscores, query, preferred_element_type=jnp.float32)
+        dk_acc[part(j)] = dk if first_k else dk_acc[part(j)] + dk
         dq = lax.dot_general(dscores, keys, TN, preferred_element_type=jnp.float32)
-        dv_acc[part(j)] = dv if first_k else dv_acc[part(j)] + dv
-        dk_acc[part(j)] = dk if first_k else dk_acc[part(j)] + dk
         dq_acc[part(s)] = dq if first_q else dq_acc[part(s)] + dq
+
+    def send_dq(n, s, peer):
+        dq_send[s - 1] = dq_acc[part(s)].astype(jnp.bfloat16)
+        return send(n, dq_send.at[s - 1], dq_recv.at[s - 1], peer)
+
+    def send_kv(n, i, acc):
+        kv_send[i] = acc[part(1)].astype(jnp.bfloat16)
+        return send(n, kv_send.at[i], kv_recv.at[i], to_y)
+
+    stores = []
+
+    def store(n, dst):
+        copy = pltpu.make_async_copy(stage.at[n], dst, store_sem.at[n])
+        copy.start()
+        stores.append(copy)
 
     tile(0, 0, True, True)
     q_c.wait_recv()
@@ -229,36 +256,46 @@
     v_y.wait_recv()
     tile(1, 0, False, True)
     tile(1, 1, False, False)
-    qc_send[0] = dq_acc[part(1)].astype(jnp.bfloat16)
-    dq_c0 = send(11, qc_send.at[0], qc_recv.at[0], to_core)
+    dq_1 = send_dq(11, 1, to_core)
     st_x.wait_recv()
     tile(1, 2, True, False)
+    tile(0, 2, False, False)
+    dq_2 = send_dq(12, 2, to_x)
     q_r.wait_recv()
     g_r.wait_recv()
     st_b.wait_recv()
-    tile(1, 3, True, False)
-    kv_send[0] = dv_acc[part(1)].astype(jnp.bfloat16)
-    dv_y = send(12, kv_send.at[0], kv_recv.at[0], to_y)
-    kv_send[1] = dk_acc[part(1)].astype(jnp.bfloat16)
-    dk_y = send(13, kv_send.at[1], kv_recv.at[1], to_y)
+    late = []
+    tile(1, 3, True, False, lambda: late.append(send_kv(13, 0, dv_acc)))
+    late.append(send_kv(14, 1, dk_acc))
     tile(0, 3, False, False)
-    qc_send[1] = dq_acc[part(3)].astype(jnp.bfloat16)
-    dq_c1 = send(14, qc_send.at[1], qc_recv.at[1], to_core)
-    tile(0, 2, False, False)
-    dq_c1.wait_recv()
-    qx_send[...] = (dq_acc[part(2)] + qc_recv[1].astype(jnp.float32)).astype(jnp.bfloat16)
-    dq_x = send(15, qx_send, qx_recv, to_x)
-    dq_c0.wait_recv()
-    dq_mine = dq_acc[part(0)] + qc_recv[0].astype(jnp.float32)
-    dv_y.wait_recv()
-    dv_out[...] = (dv_acc[part(0)] + kv_recv[0].astype(jnp.float32)).astype(jnp.bfloat16)
-    dk_y.wait_recv()
-    dk_out[...] = (
+    dq_3 = send_dq(15, 3, to_both)
+    dq_1.wait_recv()
+    dq_2.wait_recv()
+    dq_mine = (dq_acc[part(0)] + dq_recv[0].astype(jnp.float32)) + dq_recv[1].astype(jnp.float32)
+    late[0].wait_recv()
+    stage[2] = (dv_acc[part(0)] + kv_recv[0].astype(jnp.float32)).astype(jnp.bfloat16)
+    store(2, dv_out)
+    late[1].wait_recv()
+    stage[1] = (
         (dk_acc[part(0)] + kv_recv[1].astype(jnp.float32)) * factor).astype(jnp.bfloat16)
-    dq_x.wait_recv()
-    dq_out[...] = ((dq_mine + qx_recv[...].astype(jnp.float32)) * factor).astype(jnp.bfloat16)
+    store(1, dk_out)
+    dq_3.wait_recv()
+    stage[0] = ((dq_mine + dq_recv[2].astype(jnp.float32)) * factor).astype(jnp.bfloat16)
+    store(0, dq_out)
     for copy in sends:
         copy.wait_send()
+    for copy in stores:
+        copy.wait()
+
+
+def store_kernel(dq_in, dk_in, dv_in, dq_out, dk_out, dv_out, sems):
+    copies = []
+    for n, (src, dst) in enumerate(((dq_in, dq_out), (dk_in, dk_out), (dv_in, dv_out))):
+        copy = pltpu.make_async_copy(src, dst, sems.at[n])
+        copy.start()
+        copies.append(copy)
+    for copy in copies:
+        copy.wait()
 
 
 def plane_body(queries, key_rows, value_rows, outputs, out_grad, saved_lse, fold_map):
@@ -266,11 +303,11 @@
     factor = 1.0 / math.sqrt(width)
     low, full = jnp.bfloat16, jnp.float32
     grad = jax.ShapeDtypeStruct((rows, width), low)
-    return pl.pallas_call(
+    grads = pl.pallas_call(
         functools.partial(plane_kernel, rows, factor),
         out_shape=(grad, grad, grad),
         in_specs=[pl.BlockSpec(memory_space=pl.ANY)] * 7,
-        out_specs=[pl.BlockSpec(memory_space=pltpu.VMEM)] * 3,
+        out_specs=[pl.BlockSpec(memory_space=pl.ANY)] * 3,
         scratch_shapes=[
             pltpu.VMEM((4 * rows, width), low),
             pltpu.VMEM((4 * rows, width), low),
@@ -285,16 +322,16 @@
             pltpu.VMEM((2 * rows, width), full),
             pltpu.VMEM((2, rows, width), low),
             pltpu.VMEM((2, rows, width), low),
-            pltpu.VMEM((2, rows, width), low),
-            pltpu.VMEM((2, rows, width), low),
-            pltpu.VMEM((rows, width), low),
-            pltpu.VMEM((rows, width), low),
+            pltpu.VMEM((3, rows, width), low),
+            pltpu.VMEM((3, rows, width), low),
+            pltpu.VMEM((3, rows, width), low),
+            pltpu.SemaphoreType.DMA((3,)),
             pltpu.SemaphoreType.DMA((7,)),
             pltpu.SemaphoreType.DMA((16,)),
             pltpu.SemaphoreType.DMA((16,)),
         ],
         compiler_params=pltpu.CompilerParams(
-            collective_id=0, has_side_effects=True, vmem_limit_bytes=32 * 2**20
+            collective_id=0, has_side_effects=True, vmem_limit_bytes=60 * 2**20
         ),
         cost_estimate=pl.CostEstimate(
             flops=80 * rows * rows * width,
@@ -302,6 +339,14 @@
             transcendentals=8 * rows * rows,
         ),
     )(queries, key_rows, value_rows, outputs, out_grad, saved_lse.reshape(1, rows), fold_map)
+    return pl.pallas_call(
+        store_kernel,
+        out_shape=(grad, grad, grad),
+        in_specs=[pl.BlockSpec(memory_space=pl.ANY)] * 3,
+        out_specs=[pl.BlockSpec(memory_space=pl.ANY)] * 3,
+        scratch_shapes=[pltpu.SemaphoreType.DMA((3,))],
+        compiler_params=pltpu.CompilerParams(vmem_limit_bytes=60 * 2**20),
+    )(*grads)
 
 
 def solution(mesh):

time: 23.3 us -> 23.4 us (level); the launches traced: 22.9 us -> 23.3 us
  Pallas kernels: 15.5 us -> 22.6 us
  local copies, waits for them, and re-layouts: 6.76 us -> 0 us
    pallas_call x0 -> x1, Pallas kernels: none -> 7.09 us  [plane_body(): pl.pallas_call(store_kernel, out_shape=(grad, grad, grad), in_specs=[pl.B...]
    unnamed x17 -> x0, local copies, waits for them, and re-layouts: 6.76 us -> none
where the time goes in v2:
time: 23.4 us; the launch traced here: 23.3 us
  Pallas kernels  22.6 us (97%)
  between operations  0.64 us (3%)
    pallas_call x1, Pallas kernels, plane_body(): pl.pallas_call(functools.partial(plane_kernel, rows, factor), out_shape=(...  15.5 us
    pallas_call x1, Pallas kernels, plane_body(): pl.pallas_call(store_kernel, out_shape=(grad, grad, grad), in_specs=[pl.B...  7.09 us

profile of v2, /device:TPU:0, one launch (start us, length us, event | category | flops | bytes accessed | tf_op | source)
XLA Modules:
  0.0 23.3 jit_solution(2399445923530325468)
XLA Ops:
  0.6 15.5 %shard_map.94 = (bf16[256,128]{1,0:T(8,128)(2,1)}, bf16[256,128]{1,0:T(8,128)(2,1)}, bf16[256,128]{1,0:T(8,128)(2,1)}) custom-call(bf16[256,128]{1,0:T(8,128)(2,1)} %q_in.1, bf16[256,128]{1,0:T(8,128)(2,1)} %k_in.1, bf16[256,128]{1,0:T(8,128)(2,1)} %v_in.1, bf16[256,128]{1,0:T(8,128)(2,1)} %o_in.1, bf16[256,128]{1,0:T(8,128)(2,1)} %g_in.1, ...), custom_call_target="tpu_custom_call" | custom-call | flops 671088640 | bytes 524288 | tf_op jit(solution)/shard_map/pallas_call | solution.py:306
  16.2 7.1 %shard_map.95 = (bf16[256,128]{1,0:T(8,128)(2,1)}, bf16[256,128]{1,0:T(8,128)(2,1)}, bf16[256,128]{1,0:T(8,128)(2,1)}) custom-call(bf16[256,128]{1,0:T(8,128)(2,1)} %get-tuple-element.6.dq_in, bf16[256,128]{1,0:T(8,128)(2,1)} %get-tuple-element.7.dk_in, bf16[256,128]{1,0:T(8,128)(2,1)} %get-tuple-element.8.dv_in), custom_call_target="tpu_custom_call" | custom-call | tf_op jit(solution)/shard_map/pallas_call | solution.py:342

commit v3 on v2

--- a/solution.py
+++ b/solution.py
@@ -125,7 +125,7 @@
     q_buf, g_buf, k_buf, v_buf, o_buf, lse_buf, map_buf, stat,
     dq_acc, dk_acc, dv_acc,
     kv_send, kv_recv, dq_send, dq_recv,
-    stage, store_sem, local_sem, send_sem, recv_sem,
+    local_sem, send_sem, recv_sem,
 ):
     p = lax.axis_index("pb")
     x = lax.axis_index("ka")
@@ -235,13 +235,6 @@
     def send_kv(n, i, acc):
         kv_send[i] = acc[part(1)].astype(jnp.bfloat16)
         return send(n, kv_send.at[i], kv_recv.at[i], to_y)
-
-    stores = []
-
-    def store(n, dst):
-        copy = pltpu.make_async_copy(stage.at[n], dst, store_sem.at[n])
-        copy.start()
-        stores.append(copy)
 
     tile(0, 0, True, True)
     q_c.wait_recv()
@@ -273,19 +266,14 @@
     dq_2.wait_recv()
     dq_mine = (dq_acc[part(0)] + dq_recv[0].astype(jnp.float32)) + dq_recv[1].astype(jnp.float32)
     late[0].wait_recv()
-    stage[2] = (dv_acc[part(0)] + kv_recv[0].astype(jnp.float32)).astype(jnp.bfloat16)
-    store(2, dv_out)
+    dv_out[...] = (dv_acc[part(0)] + kv_recv[0].astype(jnp.float32)).astype(jnp.bfloat16)
     late[1].wait_recv()
-    stage[1] = (
+    dk_out[...] = (
         (dk_acc[part(0)] + kv_recv[1].astype(jnp.float32)) * factor).astype(jnp.bfloat16)
-    store(1, dk_out)
     dq_3.wait_recv()
-    stage[0] = ((dq_mine + dq_recv[2].astype(jnp.float32)) * factor).astype(jnp.bfloat16)
-    store(0, dq_out)
+    dq_out[...] = ((dq_mine + dq_recv[2].astype(jnp.float32)) * factor).astype(jnp.bfloat16)
     for copy in sends:
         copy.wait_send()
-    for copy in stores:
-        copy.wait()
 
 
 def store_kernel(dq_in, dk_in, dv_in, dq_out, dk_out, dv_out, sems):
@@ -303,11 +291,16 @@
     factor = 1.0 / math.sqrt(width)
     low, full = jnp.bfloat16, jnp.float32
     grad = jax.ShapeDtypeStruct((rows, width), low)
+    arrays = [
+        pltpu.with_memory_space_constraint(a, pltpu.HBM)
+        for a in (queries, key_rows, value_rows, outputs, out_grad, saved_lse.reshape(1, rows),
+                  fold_map)
+    ]
     grads = pl.pallas_call(
         functools.partial(plane_kernel, rows, factor),
-        out_shape=(grad, grad, grad),
+        out_shape=(pltpu.VMEM((rows, width), low),) * 3,
         in_specs=[pl.BlockSpec(memory_space=pl.ANY)] * 7,
-        out_specs=[pl.BlockSpec(memory_space=pl.ANY)] * 3,
+        out_specs=[pl.BlockSpec(memory_space=pltpu.VMEM)] * 3,
         scratch_shapes=[
             pltpu.VMEM((4 * rows, width), low),
             pltpu.VMEM((4 * rows, width), low),
@@ -324,28 +317,25 @@
             pltpu.VMEM((2, rows, width), low),
             pltpu.VMEM((3, rows, width), low),
             pltpu.VMEM((3, rows, width), low),
-            pltpu.VMEM((3, rows, width), low),
-            pltpu.SemaphoreType.DMA((3,)),
             pltpu.SemaphoreType.DMA((7,)),
             pltpu.SemaphoreType.DMA((16,)),
             pltpu.SemaphoreType.DMA((16,)),
         ],
         compiler_params=pltpu.CompilerParams(
-            collective_id=0, has_side_effects=True, vmem_limit_bytes=60 * 2**20
+            collective_id=0, has_side_effects=True, vmem_limit_bytes=32 * 2**20
         ),
         cost_estimate=pl.CostEstimate(
             flops=80 * rows * rows * width,
             bytes_accessed=16 * rows * width,
             transcendentals=8 * rows * rows,
         ),
-    )(queries, key_rows, value_rows, outputs, out_grad, saved_lse.reshape(1, rows), fold_map)
+    )(*arrays)
     return pl.pallas_call(
         store_kernel,
         out_shape=(grad, grad, grad),
         in_specs=[pl.BlockSpec(memory_space=pl.ANY)] * 3,
         out_specs=[pl.BlockSpec(memory_space=pl.ANY)] * 3,
         scratch_shapes=[pltpu.SemaphoreType.DMA((3,))],
-        compiler_params=pltpu.CompilerParams(vmem_limit_bytes=60 * 2**20),
     )(*grads)
 
 

time: 23.4 us -> 24.6 us (1.051)
  local copies, waits for them, and re-layouts: 0 us -> 1.84 us
  Pallas kernels: 22.6 us -> 22 us
    unnamed x0 -> x6, local copies, waits for them, and re-layouts: none -> 1.84 us
    pallas_call x1, Pallas kernels: 15.5 us -> 14.9 us  [plane_body(): pl.pallas_call(functools.partial(plane_kernel, rows, factor), out_shape=(...]
where the time goes in v3:
time: 24.6 us; the launch traced here: 24.5 us
  Pallas kernels  22 us (89%)
  local copies, waits for them, and re-layouts  1.84 us (7%)
  between operations  0.65 us (3%)
    pallas_call x1, Pallas kernels, plane_body(): pl.pallas_call(functools.partial(plane_kernel, rows, factor), out_shape=(...  14.9 us
    pallas_call x1, Pallas kernels, plane_body(): pl.pallas_call(store_kernel, out_shape=(grad, grad, grad), in_specs=[pl.B...  7.08 us
    unnamed x6, local copies, waits for them, and re-layouts  1.84 us

profile of v3, /device:TPU:0, one launch (start us, length us, event | category | flops | bytes accessed | tf_op | source)
XLA Modules:
  0.0 24.5 jit_solution(7509602328538426116)
XLA Ops:
  0.6 14.9 %shard_map.94 = (bf16[256,128]{1,0:T(8,128)(2,1)S(1)}, bf16[256,128]{1,0:T(8,128)(2,1)S(1)}, bf16[256,128]{1,0:T(8,128)(2,1)S(1)}) custom-call(bf16[256,128]{1,0:T(8,128)(2,1)} %q_in.1, bf16[256,128]{1,0:T(8,128)(2,1)} %k_in.1, bf16[256,128]{1,0:T(8,128)(2,1)} %v_in.1, bf16[256,128]{1,0:T(8,128)(2,1)} %o_in.1, bf16[256,128]{1,0:T(8,128)(2,1)} %g_in.1, ...), custom_call_target="tpu_custom_call" | custom-call | flops 671088640 | bytes 524288 | tf_op jit(solution)/shard_map/pallas_call | solution.py:299
  15.5 0.0 copy-start
  15.6 0.6 %copy-done = bf16[256,128]{1,0:T(8,128)(2,1)} copy-done((bf16[256,128]{1,0:T(8,128)(2,1)}, bf16[256,128]{1,0:T(8,128)(2,1)S(1)}, u32[]{:S(2)}) %copy-start) | copy-done | bytes 65560
  16.2 0.0 copy-start.1
  16.2 0.6 %copy-done.1 = bf16[256,128]{1,0:T(8,128)(2,1)} copy-done((bf16[256,128]{1,0:T(8,128)(2,1)}, bf16[256,128]{1,0:T(8,128)(2,1)S(1)}, u32[]{:S(2)}) %copy-start.1) | copy-done | bytes 65560
  16.8 0.0 copy-start.2
  16.8 0.6 %copy-done.2 = bf16[256,128]{1,0:T(8,128)(2,1)} copy-done((bf16[256,128]{1,0:T(8,128)(2,1)}, bf16[256,128]{1,0:T(8,128)(2,1)S(1)}, u32[]{:S(2)}) %copy-start.2) | copy-done | bytes 65560
  17.4 7.1 %shard_map.95 = (bf16[256,128]{1,0:T(8,128)(2,1)}, bf16[256,128]{1,0:T(8,128)(2,1)}, bf16[256,128]{1,0:T(8,128)(2,1)}) custom-call(bf16[256,128]{1,0:T(8,128)(2,1)} %copy-done, bf16[256,128]{1,0:T(8,128)(2,1)} %copy-done.1, bf16[256,128]{1,0:T(8,128)(2,1)} %copy-done.2), custom_call_target="tpu_custom_call" | custom-call | tf_op jit(solution)/shard_map/pallas_call | solution.py:333
Async XLA Ops:
  15.5 0.6 %copy-start = (bf16[256,128]{1,0:T(8,128)(2,1)}, bf16[256,128]{1,0:T(8,128)(2,1)S(1)}, u32[]{:S(2)}) copy-start(bf16[256,128]{1,0:T(8,128)(2,1)S(1)} %get-tuple-element.6.dq_in) | copy-start | bytes 196612
  16.2 0.6 %copy-start.1 = (bf16[256,128]{1,0:T(8,128)(2,1)}, bf16[256,128]{1,0:T(8,128)(2,1)S(1)}, u32[]{:S(2)}) copy-start(bf16[256,128]{1,0:T(8,128)(2,1)S(1)} %get-tuple-element.7.dk_in) | copy-start | bytes 196612
  16.8 0.6 %copy-start.2 = (bf16[256,128]{1,0:T(8,128)(2,1)}, bf16[256,128]{1,0:T(8,128)(2,1)S(1)}, u32[]{:S(2)}) copy-start(bf16[256,128]{1,0:T(8,128)(2,1)S(1)} %get-tuple-element.8.dv_in) | copy-start | bytes 196612

commit v4 on v3

--- a/solution.py
+++ b/solution.py
@@ -143,6 +143,9 @@
     def part(slot):
         return pl.ds(slot * rows, rows)
 
+    barrier = pltpu.get_barrier_semaphore()
+    for peer in (to_core, to_x, to_y, to_both):
+        pl.semaphore_signal(barrier, inc=1, device_id=peer, device_id_type=MESH)
     locals_ = []
     for n, (src, dst) in enumerate((
         (g_in, g_buf.at[part(0)]), (o_in, o_buf), (lse_in, lse_buf), (q_in, q_buf.at[part(0)]),
@@ -151,10 +154,6 @@
         copy = pltpu.make_async_copy(src, dst, local_sem.at[n])
         copy.start()
         locals_.append(copy)
-
-    barrier = pltpu.get_barrier_semaphore()
-    for peer in (to_core, to_x, to_y, to_both):
-        pl.semaphore_signal(barrier, inc=1, device_id=peer, device_id_type=MESH)
     pl.semaphore_wait(barrier, 4)
 
     sends = []
@@ -198,35 +197,52 @@
     lane = lax.broadcasted_iota(jnp.int32, (fold_rows, rows), 1) % fold_rows
     level = lax.broadcasted_iota(jnp.int32, (fold_rows, rows), 0)
 
-    def probabilities(j, s, scores):
-        q_fold = jnp.where(half == 0, map_buf[q_owner[s] * 2], map_buf[q_owner[s] * 2 + 1])
-        lse_row = stat[s, 0:1, :]
+    def span(slots):
+        return pl.ds(slots[0] * rows, len(slots) * rows)
+
+    def stat_row(n, slots):
+        return jnp.concatenate([stat[s, n:n + 1, :] for s in slots], axis=1)
+
+    def probabilities(keyed, asked, scores):
+        own = keyed == [0] and asked == [0]
+        q_fold = jnp.concatenate([
+            jnp.where(half == 0, map_buf[q_owner[s] * 2], map_buf[q_owner[s] * 2 + 1])
+            for s in asked], axis=1)
+        lse_row = stat_row(0, asked)
         parts = []
-        for i in range(2):
-            k_fold = map_buf[k_owner[j] * 2 + i]
-            scaled = scores[i * fold_rows:(i + 1) * fold_rows] * (factor * log2e)
-            if j == 0 and s == 0:
+        for n in range(2 * len(keyed)):
+            k_fold = map_buf[k_owner[keyed[n // 2]] * 2 + n % 2]
+            scaled = scores[n * fold_rows:(n + 1) * fold_rows] * (factor * log2e)
+            if own:
                 seen = k_fold * fold_rows + level <= q_fold * fold_rows + lane
                 parts.append(jnp.where(seen, jnp.exp2(scaled - lse_row), 0.0))
             else:
                 parts.append(jnp.exp2(scaled - jnp.where(q_fold > k_fold, lse_row, 1e30)))
-        return jnp.concatenate(parts, axis=0)
-
-    def tile(j, s, first_q, first_k, after_dv=None):
-        keys, values = k_buf[part(j)], v_buf[part(j)]
-        query, grad = q_buf[part(s)], g_buf[part(s)]
-        scores = lax.dot_general(keys, query, NT, preferred_element_type=jnp.float32)
-        dprobs = lax.dot_general(values, grad, NT, preferred_element_type=jnp.float32)
-        probs = probabilities(j, s, scores)
-        dv = jnp.dot(probs.astype(jnp.bfloat16), grad, preferred_element_type=jnp.float32)
-        dv_acc[part(j)] = dv if first_k else dv_acc[part(j)] + dv
-        if after_dv is not None:
-            after_dv()
-        dscores = (probs * (dprobs - stat[s, 1:2, :])).astype(jnp.bfloat16)
-        dk = jnp.dot(dscores, query, preferred_element_type=jnp.float32)
-        dk_acc[part(j)] = dk if first_k else dk_acc[part(j)] + dk
-        dq = lax.dot_general(dscores, keys, TN, preferred_element_type=jnp.float32)
-        dq_acc[part(s)] = dq if first_q else dq_acc[part(s)] + dq
+        return parts
+
+    def tile(keyed, asked, first_q, first_k, after_dv=None, after_dk=None):
+        query, grad = q_buf[span(asked)], g_buf[span(asked)]
+        scores = lax.dot_general(k_buf[span(keyed)], query, NT, preferred_element_type=jnp.float32)
+        dprobs = lax.dot_general(v_buf[span(keyed)], grad, NT, preferred_element_type=jnp.float32)
+        parts = probabilities(keyed, asked, scores)
+        delta_row = stat_row(1, asked)
+        lows = []
+        for n in reversed(range(len(keyed))):
+            j = keyed[n]
+            probs = jnp.concatenate(parts[2 * n:2 * n + 2], axis=0)
+            dv = jnp.dot(probs.astype(jnp.bfloat16), grad, preferred_element_type=jnp.float32)
+            dv_acc[part(j)] = dv if first_k else dv_acc[part(j)] + dv
+            if after_dv is not None and j == 1:
+                after_dv()
+            dscores = probs * (dprobs[n * rows:(n + 1) * rows] - delta_row)
+            lows.insert(0, dscores.astype(jnp.bfloat16))
+            dk = jnp.dot(lows[0], query, preferred_element_type=jnp.float32)
+            dk_acc[part(j)] = dk if first_k else dk_acc[part(j)] + dk
+            if after_dk is not None and j == 1:
+                after_dk()
+        low = jnp.concatenate(lows, axis=0)
+        dq = lax.dot_general(low, k_buf[span(keyed)], TN, preferred_element_type=jnp.float32)
+        dq_acc[span(asked)] = dq if first_q else dq_acc[span(asked)] + dq
 
     def send_dq(n, s, peer):
         dq_send[s - 1] = dq_acc[part(s)].astype(jnp.bfloat16)
@@ -236,31 +252,28 @@
         kv_send[i] = acc[part(1)].astype(jnp.bfloat16)
         return send(n, kv_send.at[i], kv_recv.at[i], to_y)
 
-    tile(0, 0, True, True)
+    tile([0], [0], True, True)
     q_c.wait_recv()
     g_c.wait_recv()
     st_c.wait_recv()
-    tile(0, 1, True, False)
+    tile([0], [1], True, False)
     q_x.wait_recv()
     q_r = send(9, q_buf.at[part(2)], q_buf.at[part(3)], to_core)
-    k_y.wait_recv()
     g_x.wait_recv()
     g_r = send(10, g_buf.at[part(2)], g_buf.at[part(3)], to_core)
+    k_y.wait_recv()
     v_y.wait_recv()
-    tile(1, 0, False, True)
-    tile(1, 1, False, False)
+    tile([1], [0, 1], False, True)
     dq_1 = send_dq(11, 1, to_core)
     st_x.wait_recv()
-    tile(1, 2, True, False)
-    tile(0, 2, False, False)
+    tile([0, 1], [2], True, False)
     dq_2 = send_dq(12, 2, to_x)
     q_r.wait_recv()
     g_r.wait_recv()
     st_b.wait_recv()
     late = []
-    tile(1, 3, True, False, lambda: late.append(send_kv(13, 0, dv_acc)))
-    late.append(send_kv(14, 1, dk_acc))
-    tile(0, 3, False, False)
+    tile([0, 1], [3], True, False, lambda: late.append(send_kv(13, 0, dv_acc)),
+         lambda: late.append(send_kv(14, 1, dk_acc)))
     dq_3 = send_dq(15, 3, to_both)
     dq_1.wait_recv()
     dq_2.wait_recv()
@@ -336,7 +349,8 @@
         in_specs=[pl.BlockSpec(memory_space=pl.ANY)] * 3,
         out_specs=[pl.BlockSpec(memory_space=pl.ANY)] * 3,
         scratch_shapes=[pltpu.SemaphoreType.DMA((3,))],
-    )(*grads)
+        compiler_params=pltpu.CompilerParams(vmem_limit_bytes=2**20),
+    )(*[pltpu.with_memory_space_constraint(a, pltpu.VMEM) for a in grads])
 
 
 def solution(mesh):

time: 24.6 us -> 16.5 us (0.67)
  Pallas kernels: 22 us -> 15.7 us
  local copies, waits for them, and re-layouts: 1.84 us -> 0 us
    pallas_call x1, Pallas kernels: 7.08 us -> 0.7 us  [plane_body(): pl.pallas_call(store_kernel, out_shape=(grad, grad, grad), in_specs=[pl.B...]
    unnamed x6 -> x0, local copies, waits for them, and re-layouts: 1.84 us -> none
where the time goes in v4:
time: 16.5 us; the launch traced here: 16.3 us
  Pallas kernels  15.7 us (95%)
  between operations  0.64 us (4%)
    pallas_call x1, Pallas kernels, plane_body(): pl.pallas_call(functools.partial(plane_kernel, rows, factor), out_shape=(...  15 us
    pallas_call x1, Pallas kernels, plane_body(): pl.pallas_call(store_kernel, out_shape=(grad, grad, grad), in_specs=[pl.B...  0.7 us

profile of v4, /device:TPU:0, one launch (start us, length us, event | category | flops | bytes accessed | tf_op | source)
XLA Modules:
  0.0 16.3 jit_solution(1936984273671378370)
XLA Ops:
  0.6 15.0 %shard_map.94 = (bf16[256,128]{1,0:T(8,128)(2,1)S(1)}, bf16[256,128]{1,0:T(8,128)(2,1)S(1)}, bf16[256,128]{1,0:T(8,128)(2,1)S(1)}) custom-call(bf16[256,128]{1,0:T(8,128)(2,1)} %q_in.1, bf16[256,128]{1,0:T(8,128)(2,1)} %k_in.1, bf16[256,128]{1,0:T(8,128)(2,1)} %v_in.1, bf16[256,128]{1,0:T(8,128)(2,1)} %o_in.1, bf16[256,128]{1,0:T(8,128)(2,1)} %g_in.1, ...), custom_call_target="tpu_custom_call" | custom-call | flops 671088640 | bytes 524288 | tf_op jit(solution)/shard_map/pallas_call | solution.py:312
  15.6 0.7 %shard_map.95 = (bf16[256,128]{1,0:T(8,128)(2,1)}, bf16[256,128]{1,0:T(8,128)(2,1)}, bf16[256,128]{1,0:T(8,128)(2,1)}) custom-call(bf16[256,128]{1,0:T(8,128)(2,1)S(1)} %get-tuple-element.6.dq_in, bf16[256,128]{1,0:T(8,128)(2,1)S(1)} %get-tuple-element.7.dk_in, bf16[256,128]{1,0:T(8,128)(2,1)S(1)} %get-tuple-element.8.dv_in), custom_call_target="tpu_custom_call" | custom-call | tf_op jit(solution)/shard_map/pallas_call | solution.py:346

commit v5 on v4

--- a/solution.py
+++ b/solution.py
@@ -220,11 +220,14 @@
                 parts.append(jnp.exp2(scaled - jnp.where(q_fold > k_fold, lse_row, 1e30)))
         return parts
 
-    def tile(keyed, asked, first_q, first_k, after_dv=None, after_dk=None):
+    def score_stage(keyed, asked):
+        scores = lax.dot_general(
+            k_buf[span(keyed)], q_buf[span(asked)], NT, preferred_element_type=jnp.float32)
+        return probabilities(keyed, asked, scores)
+
+    def grad_stage(keyed, asked, parts, first_q, first_k, after_dv=None, after_dk=None):
         query, grad = q_buf[span(asked)], g_buf[span(asked)]
-        scores = lax.dot_general(k_buf[span(keyed)], query, NT, preferred_element_type=jnp.float32)
         dprobs = lax.dot_general(v_buf[span(keyed)], grad, NT, preferred_element_type=jnp.float32)
-        parts = probabilities(keyed, asked, scores)
         delta_row = stat_row(1, asked)
         lows = []
         for n in reversed(range(len(keyed))):
@@ -252,28 +255,31 @@
         kv_send[i] = acc[part(1)].astype(jnp.bfloat16)
         return send(n, kv_send.at[i], kv_recv.at[i], to_y)
 
-    tile([0], [0], True, True)
+    grad_stage([0], [0], score_stage([0], [0]), True, True)
     q_c.wait_recv()
     g_c.wait_recv()
     st_c.wait_recv()
-    tile([0], [1], True, False)
+    grad_stage([0], [1], score_stage([0], [1]), True, False)
     q_x.wait_recv()
     q_r = send(9, q_buf.at[part(2)], q_buf.at[part(3)], to_core)
+    k_y.wait_recv()
+    near = score_stage([1], [0, 1])
+    st_x.wait_recv()
+    across = score_stage([0, 1], [2])
+    q_r.wait_recv()
+    st_b.wait_recv()
+    corner = score_stage([0, 1], [3])
     g_x.wait_recv()
     g_r = send(10, g_buf.at[part(2)], g_buf.at[part(3)], to_core)
-    k_y.wait_recv()
     v_y.wait_recv()
-    tile([1], [0, 1], False, True)
+    grad_stage([1], [0, 1], near, False, True)
     dq_1 = send_dq(11, 1, to_core)
-    st_x.wait_recv()
-    tile([0, 1], [2], True, False)
+    grad_stage([0, 1], [2], across, True, False)
     dq_2 = send_dq(12, 2, to_x)
-    q_r.wait_recv()
     g_r.wait_recv()
-    st_b.wait_recv()
     late = []
-    tile([0, 1], [3], True, False, lambda: late.append(send_kv(13, 0, dv_acc)),
-         lambda: late.append(send_kv(14, 1, dk_acc)))
+    grad_stage([0, 1], [3], corner, True, False, lambda: late.append(send_kv(13, 0, dv_acc)),
+               lambda: late.append(send_kv(14, 1, dk_acc)))
     dq_3 = send_dq(15, 3, to_both)
     dq_1.wait_recv()
     dq_2.wait_recv()

time: 16.5 us -> 17 us (1.030)
  Pallas kernels: 15.7 us -> 16.2 us
    pallas_call x1, Pallas kernels: 15 us -> 15.5 us  [plane_body(): pl.pallas_call(functools.partial(plane_kernel, rows, factor), out_shape=(...]
where the time goes in v5:
time: 17 us; the launch traced here: 16.8 us
  Pallas kernels  16.2 us (95%)
  between operations  0.64 us (4%)
    pallas_call x1, Pallas kernels, plane_body(): pl.pallas_call(functools.partial(plane_kernel, rows, factor), out_shape=(...  15.5 us
    pallas_call x1, Pallas kernels, plane_body(): pl.pallas_call(store_kernel, out_shape=(grad, grad, grad), in_specs=[pl.B...  0.7 us

profile of v5, /device:TPU:0, one launch (start us, length us, event | category | flops | bytes accessed | tf_op | source)
XLA Modules:
  0.0 16.8 jit_solution(12594366566175626447)
XLA Ops:
  0.6 15.5 %shard_map.94 = (bf16[256,128]{1,0:T(8,128)(2,1)S(1)}, bf16[256,128]{1,0:T(8,128)(2,1)S(1)}, bf16[256,128]{1,0:T(8,128)(2,1)S(1)}) custom-call(bf16[256,128]{1,0:T(8,128)(2,1)} %q_in.1, bf16[256,128]{1,0:T(8,128)(2,1)} %k_in.1, bf16[256,128]{1,0:T(8,128)(2,1)} %v_in.1, bf16[256,128]{1,0:T(8,128)(2,1)} %o_in.1, bf16[256,128]{1,0:T(8,128)(2,1)} %g_in.1, ...), custom_call_target="tpu_custom_call" | custom-call | flops 671088640 | bytes 524288 | tf_op jit(solution)/shard_map/pallas_call | solution.py:318
  16.1 0.7 %shard_map.95 = (bf16[256,128]{1,0:T(8,128)(2,1)}, bf16[256,128]{1,0:T(8,128)(2,1)}, bf16[256,128]{1,0:T(8,128)(2,1)}) custom-call(bf16[256,128]{1,0:T(8,128)(2,1)S(1)} %get-tuple-element.6.dq_in, bf16[256,128]{1,0:T(8,128)(2,1)S(1)} %get-tuple-element.7.dk_in, bf16[256,128]{1,0:T(8,128)(2,1)S(1)} %get-tuple-element.8.dv_in), custom_call_target="tpu_custom_call" | custom-call | tf_op jit(solution)/shard_map/pallas_call | solution.py:352

commit v6 on v4

--- a/solution.py
+++ b/solution.py
@@ -241,11 +241,11 @@
             if after_dk is not None and j == 1:
                 after_dk()
         low = jnp.concatenate(lows, axis=0)
-        dq = lax.dot_general(low, k_buf[span(keyed)], TN, preferred_element_type=jnp.float32)
-        dq_acc[span(asked)] = dq if first_q else dq_acc[span(asked)] + dq
+        dq = lax.dot_general(k_buf[span(keyed)], low, TN, preferred_element_type=jnp.float32)
+        dq_acc[:, span(asked)] = dq if first_q else dq_acc[:, span(asked)] + dq
 
     def send_dq(n, s, peer):
-        dq_send[s - 1] = dq_acc[part(s)].astype(jnp.bfloat16)
+        dq_send[s - 1] = dq_acc[:, part(s)].astype(jnp.bfloat16)
         return send(n, dq_send.at[s - 1], dq_recv.at[s - 1], peer)
 
     def send_kv(n, i, acc):
@@ -277,14 +277,15 @@
     dq_3 = send_dq(15, 3, to_both)
     dq_1.wait_recv()
     dq_2.wait_recv()
-    dq_mine = (dq_acc[part(0)] + dq_recv[0].astype(jnp.float32)) + dq_recv[1].astype(jnp.float32)
+    dq_mine = (dq_acc[:, part(0)] + dq_recv[0].astype(jnp.float32)) + dq_recv[1].astype(jnp.float32)
     late[0].wait_recv()
     dv_out[...] = (dv_acc[part(0)] + kv_recv[0].astype(jnp.float32)).astype(jnp.bfloat16)
     late[1].wait_recv()
     dk_out[...] = (
         (dk_acc[part(0)] + kv_recv[1].astype(jnp.float32)) * factor).astype(jnp.bfloat16)
     dq_3.wait_recv()
-    dq_out[...] = ((dq_mine + dq_recv[2].astype(jnp.float32)) * factor).astype(jnp.bfloat16)
+    dq_mine = ((dq_mine + dq_recv[2].astype(jnp.float32)) * factor).T
+    dq_out[...] = dq_mine.astype(jnp.bfloat16)
     for copy in sends:
         copy.wait_send()
 
@@ -323,13 +324,13 @@
             pltpu.VMEM((1, rows), low),
             pltpu.SMEM(fold_map.shape, jnp.int32),
             pltpu.VMEM((4, 8, rows), full),
-            pltpu.VMEM((4 * rows, width), full),
+            pltpu.VMEM((width, 4 * rows), full),
             pltpu.VMEM((2 * rows, width), full),
             pltpu.VMEM((2 * rows, width), full),
             pltpu.VMEM((2, rows, width), low),
             pltpu.VMEM((2, rows, width), low),
-            pltpu.VMEM((3, rows, width), low),
-            pltpu.VMEM((3, rows, width), low),
+            pltpu.VMEM((3, width, rows), low),
+            pltpu.VMEM((3, width, rows), low),
             pltpu.SemaphoreType.DMA((7,)),
             pltpu.SemaphoreType.DMA((16,)),
             pltpu.SemaphoreType.DMA((16,)),

time: 16.5 us -> 16.6 us (level)
  no operation moved by 1% of the time
where the time goes in v6:
time: 16.6 us; the launch traced here: 16.4 us
  Pallas kernels  15.8 us (95%)
  between operations  0.64 us (4%)
    pallas_call x1, Pallas kernels, plane_body(): pl.pallas_call(functools.partial(plane_kernel, rows, factor), out_shape=(...  15.1 us
    pallas_call x1, Pallas kernels, plane_body(): pl.pallas_call(store_kernel, out_shape=(grad, grad, grad), in_specs=[pl.B...  0.7 us

profile of v6, /device:TPU:0, one launch (start us, length us, event | category | flops | bytes accessed | tf_op | source)
XLA Modules:
  0.0 16.4 jit_solution(1968550770646087924)
XLA Ops:
  0.6 15.1 %shard_map.94 = (bf16[256,128]{1,0:T(8,128)(2,1)S(1)}, bf16[256,128]{1,0:T(8,128)(2,1)S(1)}, bf16[256,128]{1,0:T(8,128)(2,1)S(1)}) custom-call(bf16[256,128]{1,0:T(8,128)(2,1)} %q_in.1, bf16[256,128]{1,0:T(8,128)(2,1)} %k_in.1, bf16[256,128]{1,0:T(8,128)(2,1)} %v_in.1, bf16[256,128]{1,0:T(8,128)(2,1)} %o_in.1, bf16[256,128]{1,0:T(8,128)(2,1)} %g_in.1, ...), custom_call_target="tpu_custom_call" | custom-call | flops 671088640 | bytes 524288 | tf_op jit(solution)/shard_map/pallas_call | solution.py:313
  15.7 0.7 %shard_map.95 = (bf16[256,128]{1,0:T(8,128)(2,1)}, bf16[256,128]{1,0:T(8,128)(2,1)}, bf16[256,128]{1,0:T(8,128)(2,1)}) custom-call(bf16[256,128]{1,0:T(8,128)(2,1)S(1)} %get-tuple-element.6.dq_in, bf16[256,128]{1,0:T(8,128)(2,1)S(1)} %get-tuple-element.7.dk_in, bf16[256,128]{1,0:T(8,128)(2,1)S(1)} %get-tuple-element.8.dv_in), custom_call_target="tpu_custom_call" | custom-call | tf_op jit(solution)/shard_map/pallas_call | solution.py:347

commit v7 on v5

--- a/solution.py
+++ b/solution.py
@@ -171,8 +171,6 @@
     k_y = send(1, k_in, k_buf.at[part(1)], to_y)
     q_c = send(2, q_in, q_buf.at[part(1)], to_core)
     g_c = send(3, g_in, g_buf.at[part(1)], to_core)
-    g_x = send(4, g_in, g_buf.at[part(2)], to_x)
-    v_y = send(5, v_in, v_buf.at[part(1)], to_y)
 
     for copy in locals_[:3]:
         copy.wait()
@@ -190,6 +188,10 @@
     st_b = send(8, stat.at[0], stat.at[3], to_both)
     for copy in locals_[3:]:
         copy.wait()
+    q_x.wait_send()
+    g_x = send(4, g_in, g_buf.at[part(2)], to_x)
+    k_y.wait_send()
+    v_y = send(5, v_in, v_buf.at[part(1)], to_y)
 
     q_owner = (p * 2 + x, p_core * 2 + x, p * 2 + 1 - x, p_core * 2 + 1 - x)
     k_owner = (p * 2 + x, p_far * 2 + x)
@@ -244,11 +246,11 @@
             if after_dk is not None and j == 1:
                 after_dk()
         low = jnp.concatenate(lows, axis=0)
-        dq = lax.dot_general(low, k_buf[span(keyed)], TN, preferred_element_type=jnp.float32)
-        dq_acc[span(asked)] = dq if first_q else dq_acc[span(asked)] + dq
+        dq = lax.dot_general(k_buf[span(keyed)], low, TN, preferred_element_type=jnp.float32)
+        dq_acc[:, span(asked)] = dq if first_q else dq_acc[:, span(asked)] + dq
 
     def send_dq(n, s, peer):
-        dq_send[s - 1] = dq_acc[part(s)].astype(jnp.bfloat16)
+        dq_send[s - 1] = dq_acc[:, part(s)].astype(jnp.bfloat16)
         return send(n, dq_send.at[s - 1], dq_recv.at[s - 1], peer)
 
     def send_kv(n, i, acc):
@@ -266,11 +268,11 @@
     near = score_stage([1], [0, 1])
     st_x.wait_recv()
     across = score_stage([0, 1], [2])
+    g_x.wait_recv()
+    g_r = send(10, g_buf.at[part(2)], g_buf.at[part(3)], to_core)
     q_r.wait_recv()
     st_b.wait_recv()
     corner = score_stage([0, 1], [3])
-    g_x.wait_recv()
-    g_r = send(10, g_buf.at[part(2)], g_buf.at[part(3)], to_core)
     v_y.wait_recv()
     grad_stage([1], [0, 1], near, False, True)
     dq_1 = send_dq(11, 1, to_core)
@@ -283,16 +285,18 @@
     dq_3 = send_dq(15, 3, to_both)
     dq_1.wait_recv()
     dq_2.wait_recv()
-    dq_mine = (dq_acc[part(0)] + dq_recv[0].astype(jnp.float32)) + dq_recv[1].astype(jnp.float32)
+    dq_mine = (dq_acc[:, part(0)] + dq_recv[0].astype(jnp.float32)) + dq_recv[1].astype(jnp.float32)
     late[0].wait_recv()
     dv_out[...] = (dv_acc[part(0)] + kv_recv[0].astype(jnp.float32)).astype(jnp.bfloat16)
     late[1].wait_recv()
     dk_out[...] = (
         (dk_acc[part(0)] + kv_recv[1].astype(jnp.float32)) * factor).astype(jnp.bfloat16)
     dq_3.wait_recv()
-    dq_out[...] = ((dq_mine + dq_recv[2].astype(jnp.float32)) * factor).astype(jnp.bfloat16)
+    dq_mine = ((dq_mine + dq_recv[2].astype(jnp.float32)) * factor).T
+    dq_out[...] = dq_mine.astype(jnp.bfloat16)
     for copy in sends:
-        copy.wait_send()
+        if copy is not q_x and copy is not k_y:
+            copy.wait_send()
 
 
 def store_kernel(dq_in, dk_in, dv_in, dq_out, dk_out, dv_out, sems):
@@ -329,13 +333,13 @@
             pltpu.VMEM((1, rows), low),
             pltpu.SMEM(fold_map.shape, jnp.int32),
             pltpu.VMEM((4, 8, rows), full),
-            pltpu.VMEM((4 * rows, width), full),
+            pltpu.VMEM((width, 4 * rows), full),
             pltpu.VMEM((2 * rows, width), full),
             pltpu.VMEM((2 * rows, width), full),
             pltpu.VMEM((2, rows, width), low),
             pltpu.VMEM((2, rows, width), low),
-            pltpu.VMEM((3, rows, width), low),
-            pltpu.VMEM((3, rows, width), low),
+            pltpu.VMEM((3, width, rows), low),
+            pltpu.VMEM((3, width, rows), low),
             pltpu.SemaphoreType.DMA((7,)),
             pltpu.SemaphoreType.DMA((16,)),
             pltpu.SemaphoreType.DMA((16,)),

time: 17 us -> 17.1 us (level)
  no operation moved by 1% of the time
where the time goes in v7:
time: 17.1 us; the launch traced here: 16.9 us
  Pallas kernels  16.3 us (95%)
  between operations  0.64 us (4%)
    pallas_call x1, Pallas kernels, plane_body(): pl.pallas_call(functools.partial(plane_kernel, rows, factor), out_shape=(...  15.6 us
    pallas_call x1, Pallas kernels, plane_body(): pl.pallas_call(store_kernel, out_shape=(grad, grad, grad), in_specs=[pl.B...  0.7 us

profile of v7, /device:TPU:0, one launch (start us, length us, event | category | flops | bytes accessed | tf_op | source)
XLA Modules:
  0.0 16.9 jit_solution(2417655819293213032)
XLA Ops:
  0.6 15.6 %shard_map.94 = (bf16[256,128]{1,0:T(8,128)(2,1)S(1)}, bf16[256,128]{1,0:T(8,128)(2,1)S(1)}, bf16[256,128]{1,0:T(8,128)(2,1)S(1)}) custom-call(bf16[256,128]{1,0:T(8,128)(2,1)} %q_in.1, bf16[256,128]{1,0:T(8,128)(2,1)} %k_in.1, bf16[256,128]{1,0:T(8,128)(2,1)} %v_in.1, bf16[256,128]{1,0:T(8,128)(2,1)} %o_in.1, bf16[256,128]{1,0:T(8,128)(2,1)} %g_in.1, ...), custom_call_target="tpu_custom_call" | custom-call | flops 671088640 | bytes 524288 | tf_op jit(solution)/shard_map/pallas_call | solution.py:322
  16.2 0.7 %shard_map.95 = (bf16[256,128]{1,0:T(8,128)(2,1)}, bf16[256,128]{1,0:T(8,128)(2,1)}, bf16[256,128]{1,0:T(8,128)(2,1)}) custom-call(bf16[256,128]{1,0:T(8,128)(2,1)S(1)} %get-tuple-element.6.dq_in, bf16[256,128]{1,0:T(8,128)(2,1)S(1)} %get-tuple-element.7.dk_in, bf16[256,128]{1,0:T(8,128)(2,1)S(1)} %get-tuple-element.8.dv_in), custom_call_target="tpu_custom_call" | custom-call | tf_op jit(solution)/shard_map/pallas_call | solution.py:356

commit v8 on v6

--- a/solution.py
+++ b/solution.py
@@ -253,14 +253,14 @@
         return send(n, kv_send.at[i], kv_recv.at[i], to_y)
 
     tile([0], [0], True, True)
+    q_x.wait_recv()
+    q_r = send(9, q_buf.at[part(2)], q_buf.at[part(3)], to_core)
+    g_x.wait_recv()
+    g_r = send(10, g_buf.at[part(2)], g_buf.at[part(3)], to_core)
     q_c.wait_recv()
     g_c.wait_recv()
     st_c.wait_recv()
     tile([0], [1], True, False)
-    q_x.wait_recv()
-    q_r = send(9, q_buf.at[part(2)], q_buf.at[part(3)], to_core)
-    g_x.wait_recv()
-    g_r = send(10, g_buf.at[part(2)], g_buf.at[part(3)], to_core)
     k_y.wait_recv()
     v_y.wait_recv()
     tile([1], [0, 1], False, True)

time: 16.6 us -> 16.6 us (level)
  no operation moved by 1% of the time
where the time goes in v8:
time: 16.6 us; the launch traced here: 16.4 us
  Pallas kernels  15.8 us (95%)
  between operations  0.64 us (4%)
    pallas_call x1, Pallas kernels, plane_body(): pl.pallas_call(functools.partial(plane_kernel, rows, factor), out_shape=(...  15.1 us
    pallas_call x1, Pallas kernels, plane_body(): pl.pallas_call(store_kernel, out_shape=(grad, grad, grad), in_specs=[pl.B...  0.7 us

profile of v8, /device:TPU:0, one launch (start us, length us, event | category | flops | bytes accessed | tf_op | source)
XLA Modules:
  0.0 16.4 jit_solution(14965261546424450242)
XLA Ops:
  0.6 15.1 %shard_map.94 = (bf16[256,128]{1,0:T(8,128)(2,1)S(1)}, bf16[256,128]{1,0:T(8,128)(2,1)S(1)}, bf16[256,128]{1,0:T(8,128)(2,1)S(1)}) custom-call(bf16[256,128]{1,0:T(8,128)(2,1)} %q_in.1, bf16[256,128]{1,0:T(8,128)(2,1)} %k_in.1, bf16[256,128]{1,0:T(8,128)(2,1)} %v_in.1, bf16[256,128]{1,0:T(8,128)(2,1)} %o_in.1, bf16[256,128]{1,0:T(8,128)(2,1)} %g_in.1, ...), custom_call_target="tpu_custom_call" | custom-call | flops 671088640 | bytes 524288 | tf_op jit(solution)/shard_map/pallas_call | solution.py:313
  15.7 0.7 %shard_map.95 = (bf16[256,128]{1,0:T(8,128)(2,1)}, bf16[256,128]{1,0:T(8,128)(2,1)}, bf16[256,128]{1,0:T(8,128)(2,1)}) custom-call(bf16[256,128]{1,0:T(8,128)(2,1)S(1)} %get-tuple-element.6.dq_in, bf16[256,128]{1,0:T(8,128)(2,1)S(1)} %get-tuple-element.7.dk_in, bf16[256,128]{1,0:T(8,128)(2,1)S(1)} %get-tuple-element.8.dv_in), custom_call_target="tpu_custom_call" | custom-call | tf_op jit(solution)/shard_map/pallas_call | solution.py:347

commit v9 on v4

--- a/solution.py
+++ b/solution.py
@@ -253,14 +253,14 @@
         return send(n, kv_send.at[i], kv_recv.at[i], to_y)
 
     tile([0], [0], True, True)
+    q_x.wait_recv()
+    q_r = send(9, q_buf.at[part(2)], q_buf.at[part(3)], to_core)
+    g_x.wait_recv()
+    g_r = send(10, g_buf.at[part(2)], g_buf.at[part(3)], to_core)
     q_c.wait_recv()
     g_c.wait_recv()
     st_c.wait_recv()
     tile([0], [1], True, False)
-    q_x.wait_recv()
-    q_r = send(9, q_buf.at[part(2)], q_buf.at[part(3)], to_core)
-    g_x.wait_recv()
-    g_r = send(10, g_buf.at[part(2)], g_buf.at[part(3)], to_core)
     k_y.wait_recv()
     v_y.wait_recv()
     tile([1], [0, 1], False, True)
@@ -272,8 +272,9 @@
     g_r.wait_recv()
     st_b.wait_recv()
     late = []
-    tile([0, 1], [3], True, False, lambda: late.append(send_kv(13, 0, dv_acc)),
+    tile([1], [3], True, False, lambda: late.append(send_kv(13, 0, dv_acc)),
          lambda: late.append(send_kv(14, 1, dk_acc)))
+    tile([0], [3], False, False)
     dq_3 = send_dq(15, 3, to_both)
     dq_1.wait_recv()
     dq_2.wait_recv()

time: 16.5 us -> 16.4 us (level)
  no operation moved by 1% of the time
where the time goes in v9:
time: 16.4 us; the launch traced here: 16.3 us
  Pallas kernels  15.6 us (95%)
  between operations  0.64 us (4%)
    pallas_call x1, Pallas kernels, plane_body(): pl.pallas_call(functools.partial(plane_kernel, rows, factor), out_shape=(...  14.9 us
    pallas_call x1, Pallas kernels, plane_body(): pl.pallas_call(store_kernel, out_shape=(grad, grad, grad), in_specs=[pl.B...  0.7 us

profile of v9, /device:TPU:0, one launch (start us, length us, event | category | flops | bytes accessed | tf_op | source)
XLA Modules:
  0.0 16.3 jit_solution(18058542092894474603)
XLA Ops:
  0.6 14.9 %shard_map.94 = (bf16[256,128]{1,0:T(8,128)(2,1)S(1)}, bf16[256,128]{1,0:T(8,128)(2,1)S(1)}, bf16[256,128]{1,0:T(8,128)(2,1)S(1)}) custom-call(bf16[256,128]{1,0:T(8,128)(2,1)} %q_in.1, bf16[256,128]{1,0:T(8,128)(2,1)} %k_in.1, bf16[256,128]{1,0:T(8,128)(2,1)} %v_in.1, bf16[256,128]{1,0:T(8,128)(2,1)} %o_in.1, bf16[256,128]{1,0:T(8,128)(2,1)} %g_in.1, ...), custom_call_target="tpu_custom_call" | custom-call | flops 671088640 | bytes 524288 | tf_op jit(solution)/shard_map/pallas_call | solution.py:313
  15.6 0.7 %shard_map.95 = (bf16[256,128]{1,0:T(8,128)(2,1)}, bf16[256,128]{1,0:T(8,128)(2,1)}, bf16[256,128]{1,0:T(8,128)(2,1)}) custom-call(bf16[256,128]{1,0:T(8,128)(2,1)S(1)} %get-tuple-element.6.dq_in, bf16[256,128]{1,0:T(8,128)(2,1)S(1)} %get-tuple-element.7.dk_in, bf16[256,128]{1,0:T(8,128)(2,1)S(1)} %get-tuple-element.8.dv_in), custom_call_target="tpu_custom_call" | custom-call | tf_op jit(solution)/shard_map/pallas_call | solution.py:347

commit v10 on v9

--- a/solution.py
+++ b/solution.py
@@ -266,14 +266,15 @@
     tile([1], [0, 1], False, True)
     dq_1 = send_dq(11, 1, to_core)
     st_x.wait_recv()
-    tile([0, 1], [2], True, False)
-    dq_2 = send_dq(12, 2, to_x)
+    tile([1], [2], True, False)
     q_r.wait_recv()
     g_r.wait_recv()
     st_b.wait_recv()
     late = []
     tile([1], [3], True, False, lambda: late.append(send_kv(13, 0, dv_acc)),
          lambda: late.append(send_kv(14, 1, dk_acc)))
+    tile([0], [2], False, False)
+    dq_2 = send_dq(12, 2, to_x)
     tile([0], [3], False, False)
     dq_3 = send_dq(15, 3, to_both)
     dq_1.wait_recv()

time: 16.4 us -> 16.4 us (level)
  no operation moved by 1% of the time
where the time goes in v10:
time: 16.4 us; the launch traced here: 16.3 us
  Pallas kernels  15.6 us (95%)
  between operations  0.64 us (4%)
    pallas_call x1, Pallas kernels, plane_body(): pl.pallas_call(functools.partial(plane_kernel, rows, factor), out_shape=(...  14.9 us
    pallas_call x1, Pallas kernels, plane_body(): pl.pallas_call(store_kernel, out_shape=(grad, grad, grad), in_specs=[pl.B...  0.7 us

profile of v10, /device:TPU:0, one launch (start us, length us, event | category | flops | bytes accessed | tf_op | source)
XLA Modules:
  0.0 16.3 jit_solution(17743422118464394631)
XLA Ops:
  0.6 14.9 %shard_map.94 = (bf16[256,128]{1,0:T(8,128)(2,1)S(1)}, bf16[256,128]{1,0:T(8,128)(2,1)S(1)}, bf16[256,128]{1,0:T(8,128)(2,1)S(1)}) custom-call(bf16[256,128]{1,0:T(8,128)(2,1)} %q_in.1, bf16[256,128]{1,0:T(8,128)(2,1)} %k_in.1, bf16[256,128]{1,0:T(8,128)(2,1)} %v_in.1, bf16[256,128]{1,0:T(8,128)(2,1)} %o_in.1, bf16[256,128]{1,0:T(8,128)(2,1)} %g_in.1, ...), custom_call_target="tpu_custom_call" | custom-call | flops 671088640 | bytes 524288 | tf_op jit(solution)/shard_map/pallas_call | solution.py:314
  15.6 0.7 %shard_map.95 = (bf16[256,128]{1,0:T(8,128)(2,1)}, bf16[256,128]{1,0:T(8,128)(2,1)}, bf16[256,128]{1,0:T(8,128)(2,1)}) custom-call(bf16[256,128]{1,0:T(8,128)(2,1)S(1)} %get-tuple-element.6.dq_in, bf16[256,128]{1,0:T(8,128)(2,1)S(1)} %get-tuple-element.7.dk_in, bf16[256,128]{1,0:T(8,128)(2,1)S(1)} %get-tuple-element.8.dv_in), custom_call_target="tpu_custom_call" | custom-call | tf_op jit(solution)/shard_map/pallas_call | solution.py:348
